TPU v7x, 32 devices: a whole 2x2x4 slice. The times are simulated.
32 devices in a mesh: groups: 2 (over y), feat: 4 (over z), trainer: 2 (over x), sub: 2 (over core).
Axes of the slice: x: 2, y: 2, z: 4, core: 2. Of those that a mesh axis runs over, the one named last changes fastest.
Arguments:
- table: bfloat16 [65536, 128], P(('groups', 'feat')), parts along dimension 0, may hold values from -6 to 6
- cur_feats: bfloat16 [81920, 128], P(('groups', 'feat', 'trainer', 'sub')), parts along dimension 0, may hold values from -6 to 6
- nbr_first: int32 [65536, 10], P(('groups', 'feat', 'trainer', 'sub')), parts along dimension 0, may hold values from 0 to 2559
- cnt_first: int32 [65536], P(('groups', 'feat', 'trainer', 'sub')), parts along dimension 0, may hold values from 1 to 10
- nbr_second: int32 [8192, 5], P(('groups', 'feat', 'trainer', 'sub')), parts along dimension 0, may hold values from 0 to 2047
- cnt_second: int32 [8192], P(('groups', 'feat', 'trainer', 'sub')), parts along dimension 0, may hold values from 1 to 5
- w1_self: bfloat16 [256, 256], P('groups'), parts along dimension 0, may hold values from -0.5 to 0.5
- w1_neigh: bfloat16 [256, 256], P('groups'), parts along dimension 0, may hold values from -0.5 to 0.5
- bias_first: float32 [512], P('groups'), parts along dimension 0, may hold values from -3 to 3
- w2_self: bfloat16 [512, 172], P('groups'), parts along dimension 0, may hold values from -0.375 to 0.375
- w2_neigh: bfloat16 [512, 172], P('groups'), parts along dimension 0, may hold values from -0.375 to 0.375
- dlogits: bfloat16 [8192, 172], P(('groups', 'feat', 'trainer', 'sub')), parts along dimension 0, may hold values from -6 to 6
- next_owner: int32 [81920, 1], P(('groups', 'feat', 'trainer', 'sub')), parts along dimension 0, may hold values from 0 to 3; in each aligned block of 2560 rows (0 to 2559, 2560 to 5119, ...) at most 1280 rows name the same one
- next_row: int32 [81920], P(('groups', 'feat', 'trainer', 'sub')), parts along dimension 0, may hold values from 0 to 8191
Outputs:
- next_feats: bfloat16 [81920, 128], P(('groups', 'feat', 'trainer', 'sub')), parts along dimension 0
- grad_w1_self: bfloat16 [256, 256], P(('groups', 'trainer', 'sub')), parts along dimension 0
- grad_w1_neigh: bfloat16 [256, 256], P(('groups', 'trainer', 'sub')), parts along dimension 0
- grad_bias_first: bfloat16 [512], P(('groups', 'trainer', 'sub')), parts along dimension 0
- grad_w2_self: bfloat16 [512, 172], P(('groups', 'trainer', 'sub')), parts along dimension 0
- grad_w2_neigh: bfloat16 [512, 172], P(('groups', 'trainer', 'sub')), parts along dimension 0
There are 2 independent parts, one for each index of `groups`. A program takes and returns all parts, laid end to end along the dimension named above; each array names one. Nothing has to cross between parts.
Inputs may be any that keep to these rules, and one draw needn't show every extreme that they name: `next_owner`: among the 2560 rows of one device, at most 1280 name the same owner, and in every draw some owner is named by exactly 1280 rows of some device. `nbr_first`: indices into the 2560 frontier rows of the same device block. `nbr_second`: indices into the 2048 destinations of the same device block.
All inputs are finite; a program needn't handle non-finite values.
Results may differ from a plain program's by a relative error of at most 0.012.
Values may be sent and summed in bfloat16 or wider, within the bound.
A program may use at most 64 MiB of HBM per device.

v0:
```python
import jax
import jax.numpy as jnp
from jax import lax
from jax.sharding import PartitionSpec as P


def tdot(left, right):
    return lax.dot_general(
        left, right, (((0,), (0,)), ((), ())), preferred_element_type=jnp.float32
    )


def mean_rows(source, index, count):
    total = jnp.zeros((index.shape[0], source.shape[1]), jnp.float32)
    for k in range(index.shape[1]):
        picked = source[index[:, k]].astype(jnp.float32)
        total = total + jnp.where((k < count)[:, None], picked, 0.0)
    return (total / count[:, None].astype(jnp.float32)).astype(jnp.bfloat16)


def owner_rank(owner, owners):
    onehot = (owner[:, None] == jnp.arange(owners, dtype=jnp.int32)[None, :]).astype(jnp.int32)
    before = jnp.cumsum(onehot, axis=0) - onehot
    return jnp.sum(before * onehot, axis=1)


def shards(
    table,
    cur_feats,
    nbr_first,
    cnt_first,
    nbr_second,
    cnt_second,
    w1_self,
    w1_neigh,
    bias_first,
    w2_self,
    w2_neigh,
    dlogits,
    next_owner,
    next_row,
):
    owners = lax.axis_size("feat")
    copies = lax.axis_size(("trainer", "sub"))
    front_rows = next_row.shape[0]
    capacity = 2 * front_rows // owners
    owner = next_owner[:, 0]
    rank = owner_rank(owner, owners)
    send = jnp.zeros((owners, capacity), jnp.int32).at[owner, rank].set(next_row)
    replies = lax.all_to_all(
        table[lax.all_to_all(send, "feat", split_axis=0, concat_axis=0, tiled=True)],
        "feat",
        split_axis=0,
        concat_axis=0,
        tiled=True,
    )
    next_feats = replies[owner, rank]
    mid_rows = nbr_first.shape[0]
    seed_rows = nbr_second.shape[0]
    factor = 1.0 / jnp.sqrt(jnp.float32(seed_rows * owners * copies))
    agg_one = mean_rows(cur_feats, nbr_first, cnt_first)
    selfrows = cur_feats[:mid_rows]
    pre = jnp.dot(selfrows, w1_self, preferred_element_type=jnp.float32)
    pre = pre + jnp.dot(agg_one, w1_neigh, preferred_element_type=jnp.float32) + bias_first
    hidden = jax.nn.silu(pre).astype(jnp.bfloat16)
    agg_two = mean_rows(hidden, nbr_second, cnt_second)
    t2s = tdot(hidden[:seed_rows], dlogits)
    t2n = tdot(agg_two, dlogits)
    dself = lax.dot_general(
        dlogits, w2_self, (((1,), (1,)), ((), ())), preferred_element_type=jnp.float32
    )
    dneigh = lax.dot_general(
        dlogits, w2_neigh, (((1,), (1,)), ((), ())), preferred_element_type=jnp.float32
    )
    dneigh = dneigh / cnt_second[:, None].astype(jnp.float32)
    dhid = jnp.zeros(pre.shape, jnp.float32).at[:seed_rows].add(dself)
    for k in range(nbr_second.shape[1]):
        dhid = dhid.at[nbr_second[:, k]].add(jnp.where((k < cnt_second)[:, None], dneigh, 0.0))
    sig = jax.nn.sigmoid(pre)
    dpre = (dhid * sig * (1.0 + pre * (1.0 - sig))).astype(jnp.bfloat16)
    t1s = tdot(selfrows, dpre)
    t1n = tdot(agg_one, dpre)
    tb1 = jnp.sum(dpre.astype(jnp.float32), axis=0)
    parts = (
        lax.psum_scatter(t1s, ("trainer", "sub"), scatter_dimension=0, tiled=True),
        lax.psum_scatter(t1n, ("trainer", "sub"), scatter_dimension=0, tiled=True),
        lax.psum_scatter(tb1, ("trainer", "sub"), scatter_dimension=0, tiled=True),
        lax.psum_scatter(t2s, ("trainer", "sub"), scatter_dimension=0, tiled=True),
        lax.psum_scatter(t2n, ("trainer", "sub"), scatter_dimension=0, tiled=True),
    )
    summed = lax.psum((parts[0], parts[1], parts[2], parts[3], parts[4]), "feat")
    grads = [(t * factor).astype(jnp.bfloat16) for t in summed]
    return (next_feats, grads[0], grads[1], grads[2], grads[3], grads[4])


def solution(mesh):
    placed = (
        P(("groups", "feat"), None),
        P(("groups", "feat", "trainer", "sub"), None),
        P(("groups", "feat", "trainer", "sub"), None),
        P(("groups", "feat", "trainer", "sub")),
        P(("groups", "feat", "trainer", "sub"), None),
        P(("groups", "feat", "trainer", "sub")),
        P("groups", None),
        P("groups", None),
        P("groups"),
        P("groups", None),
        P("groups", None),
        P(("groups", "feat", "trainer", "sub"), None),
        P(("groups", "feat", "trainer", "sub"), None),
        P(("groups", "feat", "trainer", "sub")),
    )
    return jax.shard_map(
        shards,
        mesh=mesh,
        in_specs=placed,
        out_specs=(
            P(("groups", "feat", "trainer", "sub"), None),
            P(("groups", "trainer", "sub"), None),
            P(("groups", "trainer", "sub"), None),
            P(("groups", "trainer", "sub")),
            P(("groups", "trainer", "sub"), None),
            P(("groups", "trainer", "sub"), None),
        ),
        check_vma=False,
    )
```

profile of v0, /device:TPU:0, one launch (start us, length us, event | category | flops | bytes accessed | tf_op | source)
XLA Modules:
  0.0 330.5 jit_solution(5739470456095803310)
XLA Ops:
  13.4 6.8 %gather_fusion.10 = bf16[2048,128]{1,0:T(8,128)(2,1)S(1)} fusion(bf16[2560,128]{1,0:T(8,128)(2,1)} %param.17, s32[2048]{0:T(1024)S(1)} %broadcast_clamp_fusion.2), kind=kCustom, calls=%fused_computation.10 | custom fusion | bytes 1056768 | tf_op jit(solution)/shard_map/gather | solution.py:16
  20.2 8.1 %gather_fusion.11 = bf16[2048,128]{1,0:T(8,128)(2,1)} fusion(bf16[2560,128]{1,0:T(8,128)(2,1)S(1)} %copy-done.1, s32[2048]{0:T(1024)S(1)} %broadcast_clamp_fusion.1), kind=kCustom, calls=%fused_computation.11 | custom fusion | bytes 1056768 | tf_op jit(solution)/shard_map/gather | solution.py:16
  28.3 8.0 %gather_fusion.2 = bf16[2048,128]{1,0:T(8,128)(2,1)} fusion(bf16[2560,128]{1,0:T(8,128)(2,1)S(1)} %copy-done.1, s32[2048]{0:T(1024)S(1)} %broadcast_clamp_fusion.10), kind=kCustom, calls=%fused_computation.2 | custom fusion | bytes 1056768 | tf_op jit(solution)/shard_map/gather | solution.py:16
  36.3 8.0 %gather_fusion.3 = bf16[2048,128]{1,0:T(8,128)(2,1)} fusion(bf16[2560,128]{1,0:T(8,128)(2,1)S(1)} %copy-done.1, s32[2048]{0:T(1024)S(1)} %broadcast_clamp_fusion.9), kind=kCustom, calls=%fused_computation.3 | custom fusion | bytes 1056768 | tf_op jit(solution)/shard_map/gather | solution.py:16
  44.2 8.0 %gather_fusion.4 = bf16[2048,128]{1,0:T(8,128)(2,1)} fusion(bf16[2560,128]{1,0:T(8,128)(2,1)S(1)} %copy-done.1, s32[2048]{0:T(1024)S(1)} %broadcast_clamp_fusion.8), kind=kCustom, calls=%fused_computation.4 | custom fusion | bytes 1056768 | tf_op jit(solution)/shard_map/gather | solution.py:16
  52.2 8.0 %gather_fusion.5 = bf16[2048,128]{1,0:T(8,128)(2,1)} fusion(bf16[2560,128]{1,0:T(8,128)(2,1)S(1)} %copy-done.1, s32[2048]{0:T(1024)S(1)} %broadcast_clamp_fusion.7), kind=kCustom, calls=%fused_computation.5 | custom fusion | bytes 1056768 | tf_op jit(solution)/shard_map/gather | solution.py:16
  60.2 8.0 %gather_fusion.6 = bf16[2048,128]{1,0:T(8,128)(2,1)} fusion(bf16[2560,128]{1,0:T(8,128)(2,1)S(1)} %copy-done.1, s32[2048]{0:T(1024)S(1)} %broadcast_clamp_fusion.6), kind=kCustom, calls=%fused_computation.6 | custom fusion | bytes 1056768 | tf_op jit(solution)/shard_map/gather | solution.py:16
  68.1 8.0 %gather_fusion.7 = bf16[2048,128]{1,0:T(8,128)(2,1)} fusion(bf16[2560,128]{1,0:T(8,128)(2,1)S(1)} %copy-done.1, s32[2048]{0:T(1024)S(1)} %broadcast_clamp_fusion.5), kind=kCustom, calls=%fused_computation.7 | custom fusion | bytes 1056768 | tf_op jit(solution)/shard_map/gather | solution.py:16
  76.1 8.0 %gather_fusion.8 = bf16[2048,128]{1,0:T(8,128)(2,1)} fusion(bf16[2560,128]{1,0:T(8,128)(2,1)S(1)} %copy-done.1, s32[2048]{0:T(1024)S(1)} %broadcast_clamp_fusion.4), kind=kCustom, calls=%fused_computation.8 | custom fusion | bytes 1056768 | tf_op jit(solution)/shard_map/gather | solution.py:16
  84.1 8.0 %gather_fusion.9 = bf16[2048,128]{1,0:T(8,128)(2,1)} fusion(bf16[2560,128]{1,0:T(8,128)(2,1)S(1)} %copy-done.1, s32[2048]{0:T(1024)S(1)} %broadcast_clamp_fusion.3), kind=kCustom, calls=%fused_computation.9 | custom fusion | bytes 1056768 | tf_op jit(solution)/shard_map/gather | solution.py:16
  96.4 4.9 %scatter_custom_fusion = f32[2048,256]{1,0:T(8,128)} fusion(f32[2048,256]{1,0:T(8,128)} %scatter-add.40, s32[256]{0:T(256)} %bitcast.79, f32[256,256]{1,0:T(8,128)S(1)} %convolution_divide_fusion, f32[]{:T(128)} %constant.65.clone.1, pred[256]{0:T(512)(128)(4,1)} %get-tuple-element.75), kind=kCustom, calls=%fused_computation.44 | custom fusion | flops 131072 | bytes 2360320 | tf_op jit(solution)/shard_map/scatter-add | solution.py:78
  101.3 4.9 %scatter_custom_fusion.1 = f32[2048,256]{1,0:T(8,128)} fusion(f32[2048,256]{1,0:T(8,128)} %scatter_custom_fusion, s32[256]{0:T(256)} %bitcast.77, f32[256,256]{1,0:T(8,128)S(1)} %convolution_divide_fusion, f32[]{:T(128)} %constant.65.clone.1, pred[256]{0:T(512)(128)(4,1)} %get-tuple-element.74), kind=kCustom, calls=%fused_computation.42 | custom fusion | flops 131072 | bytes 2360320 | tf_op jit(solution)/shard_map/scatter-add | solution.py:78
  106.2 4.9 %scatter_custom_fusion.2 = f32[2048,256]{1,0:T(8,128)} fusion(f32[2048,256]{1,0:T(8,128)} %scatter_custom_fusion.1, s32[256]{0:T(256)S(1)} %bitcast.75, f32[256,256]{1,0:T(8,128)S(1)} %convolution_divide_fusion, f32[]{:T(128)} %constant.65.clone.1, pred[256]{0:T(512)(128)(4,1)} %get-tuple-element.73), kind=kCustom, calls=%fused_computation.40 | custom fusion | flops 131072 | bytes 2360320 | tf_op jit(solution)/shard_map/scatter-add | solution.py:78
  111.1 4.9 %scatter_custom_fusion.3 = f32[2048,256]{1,0:T(8,128)} fusion(f32[2048,256]{1,0:T(8,128)} %scatter_custom_fusion.2, s32[256]{0:T(256)} %bitcast.73, f32[256,256]{1,0:T(8,128)S(1)} %convolution_divide_fusion, f32[]{:T(128)} %constant.65.clone.1, pred[256]{0:T(512)(128)(4,1)} %get-tuple-element.76), kind=kCustom, calls=%fused_computation.38 | custom fusion | flops 131072 | bytes 2360320 | tf_op jit(solution)/shard_map/scatter-add | solution.py:78
  116.0 4.9 %scatter_custom_fusion.4 = f32[2048,256]{1,0:T(8,128)} fusion(f32[2048,256]{1,0:T(8,128)} %scatter_custom_fusion.3, s32[256]{0:T(256)} %bitcast.71, f32[256,256]{1,0:T(8,128)S(1)} %convolution_divide_fusion, f32[]{:T(128)} %constant.65.clone.1, pred[256]{0:T(512)(128)(4,1)} %get-tuple-element.72), kind=kCustom, calls=%fused_computation.36 | custom fusion | flops 131072 | bytes 2360320 | tf_op jit(solution)/shard_map/scatter-add | solution.py:78
  120.9 7.4 %divide_convert_fusion = bf16[2048,128]{1,0:T(8,128)(2,1)S(1)} fusion(bf16[2048,128]{1,0:T(8,128)(2,1)} %gather_fusion.11, bf16[2048,128]{1,0:T(8,128)(2,1)S(1)} %gather_fusion.10, bf16[2048,128]{1,0:T(8,128)(2,1)} %gather_fusion.9, bf16[2048,128]{1,0:T(8,128)(2,1)} %gather_fusion.8, bf16[2048,128]{1,0:T(8,128)(2,1)} %gather_fusion.7, ...), kind=kLoop, calls=%fused_computation.31 | loop fusion | flops 8126464 | bytes 5795840 | tf_op jit(solution)/shard_map/convert_element_type | solution.py:18
  134.7 10.7 %scatter_custom_fusion.5 = s32[5120]{0:T(1024)} fusion(s32[2560]{0:T(1024)S(1)} %broadcast_select_fusion, s32[2560]{0:T(1024)} %param.29, s32[]{:T(128)} %constant.29.clone.1), kind=kCustom, calls=%fused_computation.90 | custom fusion | bytes 20992
  145.3 6.3 %all-to-all-start = ((s32[4,1,1280]{2,1,0:T(1,128)}), s32[4,1,1280]{2,1,0:T(1,128)S(1)}, u32[]{:S(2)}, u32[]{:S(2)}) async-start(s32[4,1,1280]{2,1,0:T(1,128)} %bitcast.1), calls=%async_computation | async-start | bytes 40960 | tf_op jit(solution)/shard_map/all_to_all | solution.py:51
  157.3 18.6 %gather_fusion = bf16[5120,128]{1,0:T(8,128)(2,1)} fusion(bf16[8192,128]{1,0:T(8,128)(2,1)S(1)} %copy-done, s32[5120]{0:T(1024)S(1)} %broadcast_clamp_fusion), kind=kCustom, calls=%fused_computation | custom fusion | bytes 2641920 | tf_op jit(solution)/shard_map/gather | solution.py:51
  192.9 5.7 %all-reduce.1 = f32[256]{0:T(256)S(1)} all-reduce(f32[256]{0:T(256)S(1)} %get-tuple-element.41), channel_id=4, replica_groups=mesh['groups'=2,'feat'=4,'trainer'=2,'sub'=2] {'trainer','sub'}, use_global_device_ids=true, to_apply=%region_14.15.clone | all-reduce | flops 256 | bytes 2048
  202.1 10.0 %reduce-scatter.11.cloned.1.call-done = f32[64,172]{1,0:T(8,128)} async-done(((f32[256,172]{1,0:T(8,128)}), f32[64,172]{1,0:T(8,128)}) %reduce-scatter.11.cloned.1.call-update) | async-done | bytes 44048 | tf_op jit(solution)/shard_map/reduce_scatter | solution.py:89
  212.1 23.1 %reduce-scatter.9.cloned.1.call-done = f32[64,172]{1,0:T(8,128)} async-done(((f32[256,172]{1,0:T(8,128)}), f32[64,172]{1,0:T(8,128)}) %reduce-scatter.9.cloned.1.call-update) | async-done | bytes 44048 | tf_op jit(solution)/shard_map/reduce_scatter | solution.py:88
  235.3 40.4 %all-reduce.5.cloned.1.call-done = (f32[32,256]{0,1:T(8,128)}, f32[32,256]{0,1:T(8,128)}, f32[64]{0:T(128)}, f32[64,172]{1,0:T(8,128)}, f32[64,172]{1,0:T(8,128)}) async-done(((f32[32,256]{0,1:T(8,128)}, f32[32,256]{0,1:T(8,128)}, f32[64]{0:T(128)}, f32[64,172]{1,0:T(8,128)}, f32[64,172]{1,0:T(8,128)}), (f32[32,256]{0,1:T(8,128)}, f32[32,256]{0,1:T(8,128)}, f32[64]{0:T(128)}, f32[64,172]{1,0:T(8,128)}, ...) | async-done | bytes 153872 | tf_op jit(solution)/shard_map/psum | solution.py:91
  280.7 43.3 %gather_fusion.1 = bf16[2560,128]{1,0:T(8,128)(2,1)} fusion(bf16[4,1280,128]{2,1,0:T(8,128)(2,1)} %all-to-all-done.1, s32[2560]{0:T(1024)S(1)} %get-tuple-element.43), kind=kCustom, calls=%fused_computation.1 | custom fusion | bytes 1331200 | tf_op jit(solution)/shard_map/gather | solution.py:57
  (137 shorter events, 47.0 us)
Async XLA Ops:
  7.2 150.2 %copy-start = (bf16[8192,128]{1,0:T(8,128)(2,1)S(1)}, bf16[8192,128]{1,0:T(8,128)(2,1)}, u32[]{:S(2)}) copy-start(bf16[8192,128]{1,0:T(8,128)(2,1)} %param.16) | copy-start | bytes 6291460
  7.2 191.9 %reduce-scatter.15.cloned.1.call-start = ((), (), s32[]{:S(2)}) async-start(), calls=%async_computation.9 | async-start | bytes 163840
  13.4 6.9 %copy-start.1 = (bf16[2560,128]{1,0:T(8,128)(2,1)S(1)}, bf16[2560,128]{1,0:T(8,128)(2,1)}, u32[]{:S(2)}) copy-start(bf16[2560,128]{1,0:T(8,128)(2,1)} %param.17) | copy-start | bytes 1966084
  84.1 8.0 %copy-start.18 = (s32[256,5]{0,1:T(8,128)S(1)}, s32[256,5]{0,1:T(8,128)}, u32[]{:S(2)}) copy-start(s32[256,5]{0,1:T(8,128)} %param.20) | copy-start | bytes 15364
  84.1 8.6 %copy-start.9 = (bf16[128,256]{1,0:T(8,128)(2,1)S(1)}, bf16[128,256]{1,0:T(8,128)(2,1)}, u32[]{:S(2)}) copy-start(bf16[128,256]{1,0:T(8,128)(2,1)} %param.22) | copy-start | bytes 196612
  92.7 13.5 %copy-start.14 = (s32[256,1]{0,1:T(1,128)}, s32[256,1]{0,1:T(1,128)S(1)}, u32[]{:S(2)}) copy-start(s32[256,1]{0,1:T(1,128)S(1)} %get-tuple-element.58) | copy-start | bytes 3076
  111.0 9.8 %copy-start.11 = (pred[2048]{0:T(1024)(128)(4,1)S(1)}, pred[2048]{0:T(1024)(128)(4,1)}, u32[]{:S(2)}) copy-start(pred[2048]{0:T(1024)(128)(4,1)} %get-tuple-element.63) | copy-start | bytes 6148
  120.8 7.5 %copy-start.3 = (f32[2048,256]{1,0:T(8,128)S(1)}, f32[2048,256]{1,0:T(8,128)}, u32[]{:S(2)}) copy-start(f32[2048,256]{1,0:T(8,128)} %scatter_custom_fusion.4) | copy-start | bytes 6291460
  120.8 7.5 %copy-start.4 = (f32[2048,256]{1,0:T(8,128)S(1)}, f32[2048,256]{1,0:T(8,128)}, u32[]{:S(2)}) copy-start(f32[2048,256]{1,0:T(8,128)} %fusion.2) | copy-start | bytes 6291460
  120.8 7.5 %copy-start.29 = (bf16[128,256]{1,0:T(8,128)(2,1)S(1)}, bf16[128,256]{1,0:T(8,128)(2,1)}, u32[]{:S(2)}) copy-start(bf16[128,256]{1,0:T(8,128)(2,1)} %param.23) | copy-start | bytes 196612
  120.9 7.5 %copy-start.30 = (f32[256]{0:T(256)S(1)}, f32[256]{0:T(256)}, u32[]{:S(2)}) copy-start(f32[256]{0:T(256)} %param.24) | copy-start | bytes 3076
  131.6 22.6 %copy-start.17 = (s32[256,1]{0,1:T(1,128)S(1)}, s32[256,1]{0,1:T(1,128)}, u32[]{:S(2)}) copy-start(s32[256,1]{0,1:T(1,128)} %get-tuple-element.60) | copy-start | bytes 3076
  131.6 22.6 %copy-start.16 = (s32[256,1]{0,1:T(1,128)S(1)}, s32[256,1]{0,1:T(1,128)}, u32[]{:S(2)}) copy-start(s32[256,1]{0,1:T(1,128)} %get-tuple-element.59) | copy-start | bytes 3076
  131.6 22.6 %copy-start.15 = (s32[256,1]{0,1:T(1,128)S(1)}, s32[256,1]{0,1:T(1,128)}, u32[]{:S(2)}) copy-start(s32[256,1]{0,1:T(1,128)} %copy-done.14) | copy-start | bytes 3076
  145.3 11.9 %all-to-all-start = ((s32[4,1,1280]{2,1,0:T(1,128)}), s32[4,1,1280]{2,1,0:T(1,128)S(1)}, u32[]{:S(2)}, u32[]{:S(2)}) async-start(s32[4,1,1280]{2,1,0:T(1,128)} %bitcast.1), calls=%async_computation | async-start | bytes 40960 | tf_op jit(solution)/shard_map/all_to_all | solution.py:51
  151.7 49.0 %reduce-scatter.13.cloned.1.call-start = ((), (), s32[]{:S(2)}) async-start(), calls=%async_computation.8 | async-start | bytes 163840
  175.9 104.7 %all-to-all-start.1 = ((bf16[4,1280,128]{2,1,0:T(8,128)(2,1)}), bf16[4,1280,128]{2,1,0:T(8,128)(2,1)}, u32[]{:S(2)}, u32[]{:S(2)}) async-start(bf16[4,1280,128]{2,1,0:T(8,128)(2,1)} %bitcast.57), calls=%async_computation.1 | async-start | bytes 2621440 | tf_op jit(solution)/shard_map/all_to_all | solution.py:50
  180.4 31.8 %reduce-scatter.11.cloned.1.call-start = ((), (), s32[]{:S(2)}) async-start(), calls=%async_computation.7 | async-start | bytes 327680 | tf_op jit(solution)/shard_map/reduce_scatter | solution.py:89
  181.6 6.6 %copy-start.7 = (bf16[256,172]{0,1:T(8,128)(2,1)S(1)}, bf16[256,172]{0,1:T(8,128)(2,1)}, u32[]{:S(2)}) copy-start(bf16[256,172]{0,1:T(8,128)(2,1)} %param.27) | copy-start | bytes 264196
  181.6 6.6 %copy-start.19 = (pred[256]{0:T(512)(128)(4,1)S(1)}, pred[256]{0:T(512)(128)(4,1)}, u32[]{:S(2)}) copy-start(pred[256]{0:T(512)(128)(4,1)} %get-tuple-element.72) | copy-start | bytes 772
  181.6 6.6 %copy-start.20 = (pred[256]{0:T(512)(128)(4,1)S(1)}, pred[256]{0:T(512)(128)(4,1)}, u32[]{:S(2)}) copy-start(pred[256]{0:T(512)(128)(4,1)} %get-tuple-element.73) | copy-start | bytes 772
  181.6 6.6 %copy-start.21 = (pred[256]{0:T(512)(128)(4,1)S(1)}, pred[256]{0:T(512)(128)(4,1)}, u32[]{:S(2)}) copy-start(pred[256]{0:T(512)(128)(4,1)} %get-tuple-element.74) | copy-start | bytes 772
  190.6 44.7 %reduce-scatter.9.cloned.1.call-start = ((), (), s32[]{:S(2)}) async-start(), calls=%async_computation.6 | async-start | bytes 327680 | tf_op jit(solution)/shard_map/reduce_scatter | solution.py:88
  191.6 84.1 %all-reduce.5.cloned.1.call-start = ((), (), s32[]{:S(2)}) async-start(), calls=%async_computation.10 | async-start | bytes 787456 | tf_op jit(solution)/shard_map/psum | solution.py:91
  (15 other events, 61.6 us)
Sparse Core Ops, SparseCore 0:
  132.7 22.2 reduce-scatter.14
  157.5 19.5 reduce-scatter.12
  190.7 21.3 reduce-scatter.10
  215.2 20.0 reduce-scatter.8
  238.4 37.2 all-reduce.4
where the time goes:
time: 332 us; the launch traced here: 330 us
  local copies, waits for them, and re-layouts  168 us (51%)
  waiting for transfers between devices  76.7 us (23%)
  other arithmetic  44.1 us (13%)
  between operations  14.9 us (4%)
  starting transfers between devices  10.9 us (3%)
  matrix products  10.3 us (3%)
  blocking collectives  5.67 us (2%)
    gather x15, local copies, waits for them, and re-layouts, mean_rows(): picked = source[index[:, k]].astype(jnp.float32)  86.4 us
    gather x1, local copies, waits for them, and re-layouts, shards(): next_feats = replies[owner, rank]  43.3 us
    psum x1, waiting for transfers between devices, shards(): lax.psum((parts[0], parts[1], parts[2], parts[3], parts[4]), 'feat')  40.4 us
    scatter-add x5, other arithmetic, shards(): dhid.at[nbr_second[:, k]]  24.4 us
    reduce_scatter x1, waiting for transfers between devices, shards(): lax.psum_scatter(t2s, ('trainer', 'sub'), scatter_dimension=0, tiled=True)  23.1 us
    gather x1, local copies, waits for them, and re-layouts, shards(): table[lax.all_to_all(send, 'feat', split_axis=0, concat_axis=0, tiled=True)]  18.6 us
    unnamed x72, local copies, waits for them, and re-layouts  18.1 us
    reduce_scatter x1, waiting for transfers between devices, shards(): lax.psum_scatter(t2n, ('trainer', 'sub'), scatter_dimension=0, tiled=True)  9.99 us
  transfers between devices with their start and end apart: 7, of which 4 were waited for; matrix products, arithmetic and copies ran while one was open for 16% of the time, Pallas kernels for 0%

commit v1 on v0

v1 whole, which is shorter than its diff:
```python
import functools

import jax
import jax.numpy as jnp
from jax import lax
from jax.experimental import pallas as pl
from jax.experimental.pallas import tpu as pltpu
from jax.sharding import PartitionSpec as P

BF = jnp.bfloat16
F32 = jnp.float32
VM = pl.BlockSpec(memory_space=pltpu.VMEM)
SM = pl.BlockSpec(memory_space=pltpu.SMEM)
MESH = pl.DeviceIdType.MESH
LANES = 128


def mm(left, right):
    return jnp.dot(left, right, preferred_element_type=F32)


def mm_nt(left, right):
    return lax.dot_general(left, right, (((1,), (1,)), ((), ())), preferred_element_type=F32)


def mm_tn(left, right):
    return lax.dot_general(left, right, (((0,), (0,)), ((), ())), preferred_element_type=F32)


def iota(shape, dim):
    return lax.broadcasted_iota(jnp.int32, shape, dim)


def route_kernel(owners, capacity, owner_ref, row_ref, slot_ref, send_ref, own_pad):
    rows = owner_ref.shape[0]
    padded = own_pad.shape[0]
    own_pad[...] = jnp.full(own_pad.shape, -1, jnp.int32)
    own_pad[0:rows, :] = owner_ref[...]
    own = own_pad[...]
    before = (iota((LANES, LANES), 0) < iota((LANES, LANES), 1)).astype(F32).astype(BF)
    every = jnp.ones((LANES, LANES), BF)
    above = (iota((padded, padded), 0) > iota((padded, padded), 1)).astype(F32).astype(BF)
    rank = jnp.zeros(own.shape, F32)
    for o in range(owners):
        named = (own == o).astype(F32)
        named16 = named.astype(BF)
        inside = mm(named16, before)
        totals = mm(named16, every).astype(BF)
        rank = rank + named * (inside + mm(above, totals))
    slot = own * capacity + rank.astype(jnp.int32)
    slot = slot[0:rows, :]
    slot_ref[...] = slot
    row = row_ref[...]
    high, low = (row >> 6).astype(F32), (row & 63).astype(F32)
    group, place = slot >> 7, slot & 127
    groups = send_ref.shape[0]
    total = jnp.zeros((2 * groups, LANES), F32)
    gid = iota((groups, LANES), 0)
    lid = iota((LANES, LANES), 0)
    for r in range(rows):
        hit = gid == group[r : r + 1, :]
        left = jnp.concatenate(
            [jnp.where(hit, high[r : r + 1, :], 0.0), jnp.where(hit, low[r : r + 1, :], 0.0)], axis=0
        ).astype(BF)
        right = (lid == place[r : r + 1, :]).astype(F32).astype(BF)
        total = total + mm_nt(left, right)
    send_ref[...] = (total[:groups] * 64.0 + total[groups:]).astype(jnp.int32)


def route(owner, row, owners, capacity):
    rows = owner.shape[0] // LANES
    padded = -(-rows // 16) * 16
    groups = owners * capacity // LANES
    return pl.pallas_call(
        functools.partial(route_kernel, owners, capacity),
        out_shape=(
            jax.ShapeDtypeStruct((rows, LANES), jnp.int32),
            jax.ShapeDtypeStruct((groups, LANES), jnp.int32),
        ),
        in_specs=[VM, VM],
        out_specs=(VM, VM),
        scratch_shapes=[pltpu.VMEM((padded, LANES), jnp.int32)],
        name="route",
    )(owner.reshape(rows, LANES), row.reshape(rows, LANES))


def take_kernel(index_ref, source_ref, out_ref, wide, picked):
    wide[...] = source_ref[...].astype(F32)
    chunk = picked.shape[0]

    @pl.loop(0, out_ref.shape[0] // chunk)
    def _(c):
        base = pl.multiple_of(c * chunk, chunk)
        for j in range(chunk):
            picked[j : j + 1, :] = wide[pl.ds(index_ref[base + j], 1), :]
        out_ref[pl.ds(base, chunk), :] = picked[...].astype(BF)


def take(source, index):
    count = index.shape[0]
    width = source.shape[1]
    chunk = 64
    return pl.pallas_call(
        take_kernel,
        out_shape=jax.ShapeDtypeStruct((count, width), BF),
        in_specs=[SM, VM],
        out_specs=VM,
        scratch_shapes=[pltpu.VMEM(source.shape, F32), pltpu.VMEM((chunk, width), F32)],
        compiler_params=pltpu.CompilerParams(vmem_limit_bytes=24 << 20),
        cost_estimate=pl.CostEstimate(flops=0, bytes_accessed=20 << 20, transcendentals=0),
        name="take_rows",
    )(index, source)


def train_kernel(
    copies,
    feats_t_ref,
    nbr1_ref,
    cnt1_ref,
    nbr2_ref,
    cnt2_ref,
    w1s_ref,
    w1n_ref,
    bias_ref,
    w2s_ref,
    w2n_ref,
    dlog_ref,
    out_ref,
    counts1,
    counts2,
    agg_t,
    z_t,
    hid_t,
):
    width, front = feats_t_ref.shape
    fan1, mid = nbr1_ref.shape
    fan2, seeds = nbr2_ref.shape
    hidden, classes = w2s_ref.shape
    chunk = seeds
    w1s_t, w1n_t = w1s_ref[...].T, w1n_ref[...].T
    bias = bias_ref[...]
    strip = 32
    one, zero = jnp.ones((strip, chunk), BF), jnp.zeros((strip, chunk), BF)
    base_row = iota((strip, chunk), 0).astype(F32)

    def strips(index_rows, valid_rows, length, put):
        for block in range(0, length, 256):
            rel = []
            for idx, ok in zip(index_rows, valid_rows):
                off = idx - block
                off = jnp.where(ok & (off >= 0) & (off < 256), off, -1).astype(F32)
                rel.append(jnp.broadcast_to(off, (strip, chunk)).astype(BF))
            for s in range(0, min(256, length - block), strip):
                rows = (base_row + float(s)).astype(BF)
                acc = jnp.where(rel[0] == rows, one, zero)
                for r in rel[1:]:
                    acc = acc + jnp.where(r == rows, one, zero)
                put(block + s, acc)

    cnt2 = cnt2_ref[...]

    def put2(at, value):
        counts2[at : at + strip, :] = value

    strips(
        [nbr2_ref[k : k + 1, :] for k in range(fan2)],
        [cnt2 > k for k in range(fan2)],
        mid,
        put2,
    )

    def put1(at, value):
        counts1[at : at + strip, :] = value

    @pl.loop(0, mid // chunk)
    def _(c):
        at = pl.ds(pl.multiple_of(c * chunk, chunk), chunk)
        cnt = cnt1_ref[:, at]
        strips([nbr1_ref[k : k + 1, at] for k in range(fan1)], [cnt > k for k in range(fan1)], front, put1)
        agg = (mm(feats_t_ref[...], counts1[...]) / cnt.astype(F32)).astype(BF)
        agg_t[:, at] = agg
        z = mm(w1s_t, feats_t_ref[:, at]) + mm(w1n_t, agg) + bias
        z_t[:, at] = z
        hid_t[:, at] = (z * jax.nn.sigmoid(z)).astype(BF)

    dlog = dlog_ref[...]
    cnt2f = cnt2.astype(F32)
    agg2_t = (mm(hid_t[...], counts2[...]) / cnt2f).astype(BF)
    t2s = mm(hid_t[:, 0:seeds], dlog)
    t2n = mm(agg2_t, dlog)
    dself_t = mm_nt(w2s_ref[...], dlog)
    dneigh_t = mm_nt(w2n_ref[...], dlog) / cnt2f
    dn_high = dneigh_t.astype(BF)
    dn_low = (dneigh_t - dn_high.astype(F32)).astype(BF)
    t1s = jnp.zeros((width, hidden), F32)
    t1n = jnp.zeros((width, hidden), F32)
    tb1 = jnp.zeros((16, hidden), F32)
    ones = jnp.ones((16, chunk), BF)
    for c in range(0, mid, chunk):
        part = counts2[c : c + chunk, :]
        dh = mm_nt(dn_high, part) + mm_nt(dn_low, part)
        if c == 0:
            dh = dh + dself_t
        z = z_t[:, c : c + chunk]
        sig = jax.nn.sigmoid(z)
        dz = (dh * sig * (1.0 + z * (1.0 - sig))).astype(BF)
        t1s = t1s + mm_nt(feats_t_ref[:, c : c + chunk], dz)
        t1n = t1n + mm_nt(agg_t[:, c : c + chunk], dz)
        tb1 = tb1 + mm_nt(ones, dz)
    r1, r2 = width // copies, hidden // copies
    for p in range(copies):
        out_ref[p, 0:r1, :] = t1s[p * r1 : (p + 1) * r1].astype(BF)
        out_ref[p, r1 : 2 * r1, :] = t1n[p * r1 : (p + 1) * r1].astype(BF)
        two = 2 * r1
        out_ref[p, two : two + 2 * r2, :] = jnp.zeros((2 * r2, hidden), BF)
        out_ref[p, two : two + r2, 0:classes] = t2s[p * r2 : (p + 1) * r2].astype(BF)
        out_ref[p, two + r2 : two + 2 * r2, 0:classes] = t2n[p * r2 : (p + 1) * r2].astype(BF)
        out_ref[p, two + 2 * r2 :, :] = tb1.astype(BF)


def train(copies, feats, nbr1, cnt1, nbr2, cnt2, w1s, w1n, bias, w2s, w2n, dlog):
    front, width = feats.shape
    mid, seeds = nbr1.shape[0], nbr2.shape[0]
    hidden = w1s.shape[1]
    rows = 2 * width // copies + 2 * hidden // copies + 16
    return pl.pallas_call(
        functools.partial(train_kernel, copies),
        out_shape=jax.ShapeDtypeStruct((copies, rows, hidden), BF),
        in_specs=[VM] * 11,
        out_specs=VM,
        scratch_shapes=[
            pltpu.VMEM((front, seeds), BF),
            pltpu.VMEM((mid, seeds), BF),
            pltpu.VMEM((width, mid), BF),
            pltpu.VMEM((hidden, mid), F32),
            pltpu.VMEM((hidden, mid), BF),
        ],
        compiler_params=pltpu.CompilerParams(vmem_limit_bytes=32 << 20),
        cost_estimate=pl.CostEstimate(flops=4 << 30, bytes_accessed=60 << 20, transcendentals=1 << 20),
        name="train",
    )(feats.T, nbr1.T, cnt1[None, :], nbr2.T, cnt2[None, :], w1s, w1n, bias[:, None], w2s, w2n, dlog)


def reduce_kernel(owners, trainers, subs, factor, in_ref, out_ref, got, part, fed, s1, r1, s2, r2):
    copies = trainers * subs
    me = lax.axis_index("trainer") * subs + lax.axis_index("sub")
    feat = lax.axis_index("feat")

    def peer(d):
        p = lax.rem(me + d, copies)
        return p, {"trainer": p // subs, "sub": lax.rem(p, subs)}

    barrier = pltpu.get_barrier_semaphore()
    for d in range(1, copies):
        pl.semaphore_signal(barrier, inc=1, device_id=peer(d)[1], device_id_type=MESH)
    for d in range(1, owners):
        pl.semaphore_signal(
            barrier, inc=1, device_id={"feat": lax.rem(feat + d, owners)}, device_id_type=MESH
        )
    pl.semaphore_wait(barrier, copies + owners - 2)
    first = []
    for d in range(1, copies):
        p, where = peer(d)
        copy = pltpu.make_async_remote_copy(
            src_ref=in_ref.at[p],
            dst_ref=got.at[d - 1],
            send_sem=s1.at[d - 1],
            recv_sem=r1.at[d - 1],
            device_id=where,
            device_id_type=MESH,
        )
        copy.start()
        first.append(copy)
    total = in_ref[me].astype(F32)
    for d in range(1, copies):
        first[d - 1].wait_recv()
        total = total + got[d - 1].astype(F32)
    part[...] = total.astype(BF)
    second = []
    for d in range(1, owners):
        copy = pltpu.make_async_remote_copy(
            src_ref=part,
            dst_ref=fed.at[feat],
            send_sem=s2.at[d - 1],
            recv_sem=r2.at[d - 1],
            device_id={"feat": lax.rem(feat + d, owners)},
            device_id_type=MESH,
        )
        copy.start()
        second.append(copy)
    fed[feat] = part[...]
    for copy in second:
        copy.wait_recv()
    total = fed[0].astype(F32)
    for f in range(1, owners):
        total = total + fed[f].astype(F32)
    out_ref[...] = (total * factor).astype(BF)
    for copy in first + second:
        copy.wait_send()


def reduce_grads(packed, owners, trainers, subs, factor):
    copies, rows, hidden = packed.shape
    return pl.pallas_call(
        functools.partial(reduce_kernel, owners, trainers, subs, factor),
        out_shape=jax.ShapeDtypeStruct((rows, hidden), BF),
        in_specs=[VM],
        out_specs=VM,
        scratch_shapes=[
            pltpu.VMEM((copies - 1, rows, hidden), BF),
            pltpu.VMEM((rows, hidden), BF),
            pltpu.VMEM((owners, rows, hidden), BF),
            pltpu.SemaphoreType.DMA((copies - 1,)),
            pltpu.SemaphoreType.DMA((copies - 1,)),
            pltpu.SemaphoreType.DMA((owners - 1,)),
            pltpu.SemaphoreType.DMA((owners - 1,)),
        ],
        compiler_params=pltpu.CompilerParams(
            collective_id=0, has_side_effects=True, vmem_limit_bytes=24 << 20
        ),
        cost_estimate=pl.CostEstimate(flops=0, bytes_accessed=40 << 20, transcendentals=0),
        name="reduce_grads",
    )(packed)


def shards(
    trainers,
    subs,
    owners,
    table,
    cur_feats,
    nbr_first,
    cnt_first,
    nbr_second,
    cnt_second,
    w1_self,
    w1_neigh,
    bias_first,
    w2_self,
    w2_neigh,
    dlogits,
    next_owner,
    next_row,
):
    copies = trainers * subs
    front_rows, width = cur_feats.shape
    hidden, classes = w2_self.shape
    capacity = 2 * front_rows // owners
    slot, send = route(next_owner[:, 0], next_row, owners, capacity)
    asked = lax.all_to_all(
        send.reshape(owners, capacity), "feat", split_axis=0, concat_axis=0, tiled=True
    )
    found = take(table, asked.reshape(-1)).reshape(owners, capacity, width)
    replies = lax.all_to_all(found, "feat", split_axis=0, concat_axis=0, tiled=True)
    packed = train(
        copies,
        cur_feats,
        nbr_first,
        cnt_first,
        nbr_second,
        cnt_second,
        w1_self,
        w1_neigh,
        bias_first,
        w2_self,
        w2_neigh,
        dlogits,
    )
    seeds_all = nbr_second.shape[0] * owners * copies
    summed = reduce_grads(packed, owners, trainers, subs, float(seeds_all) ** -0.5)
    next_feats = take(replies.reshape(-1, width), slot.reshape(-1))
    r1, r2 = width // copies, hidden // copies
    two = 2 * r1
    me = lax.axis_index("trainer") * subs + lax.axis_index("sub")
    return (
        next_feats,
        summed[0:r1],
        summed[r1:two],
        lax.dynamic_slice(summed[two + 2 * r2], (me * r2,), (r2,)),
        summed[two : two + r2, 0:classes],
        summed[two + r2 : two + 2 * r2, 0:classes],
    )


def solution(mesh):
    every = ("groups", "feat", "trainer", "sub")
    share = ("groups", "trainer", "sub")
    placed = (
        P(("groups", "feat"), None),
        P(every, None),
        P(every, None),
        P(every),
        P(every, None),
        P(every),
        P("groups", None),
        P("groups", None),
        P("groups"),
        P("groups", None),
        P("groups", None),
        P(every, None),
        P(every, None),
        P(every),
    )
    shape = mesh.shape
    return jax.shard_map(
        functools.partial(shards, shape["trainer"], shape["sub"], shape["feat"]),
        mesh=mesh,
        in_specs=placed,
        out_specs=(
            P(every, None),
            P(share, None),
            P(share, None),
            P(share),
            P(share, None),
            P(share, None),
        ),
        check_vma=False,
    )
```

time: 332 us -> 73.7 us (0.22)
  local copies, waits for them, and re-layouts: 168 us -> 4.55 us
  waiting for transfers between devices: 76.7 us -> 0.01 us
  Pallas kernels: 0 us -> 50.7 us
  other arithmetic: 44.1 us -> 1.33 us
  between operations: 14.9 us -> 0.87 us
  matrix products: 10.3 us -> 0 us
  starting transfers between devices: 10.9 us -> 3.67 us
  blocking collectives: 5.67 us -> 11.9 us
    gather x17 -> x0, local copies, waits for them, and re-layouts: 148 us -> none  [the longest x15 86.4 us: mean_rows(): picked = source[index[:, k]].astype(jnp.float32)]
    pallas_call x0 -> x5, Pallas kernels: none -> 50.7 us  [the longest x1 18.8 us: train(): pl.pallas_call(functools.partial(train_kernel, copies), out_shape=jax.Sha...]
    psum x1 -> x0, waiting for transfers between devices: 40.4 us -> none  [shards(): lax.psum((parts[0], parts[1], parts[2], parts[3], parts[4]), 'feat')]
    reduce_scatter x2 -> x0, waiting for transfers between devices: 33.1 us -> none  [the longest x1 23.1 us: shards(): lax.psum_scatter(t2s, ('trainer', 'sub'), scatter_dimension=0, tiled=True)]
    scatter-add x5 -> x0, other arithmetic: 24.4 us -> none  [shards(): dhid.at[nbr_second[:, k]]]
    unnamed x72 -> x30, local copies, waits for them, and re-layouts: 18.1 us -> 2.58 us
    convert_element_type x7 -> x0, other arithmetic: 13 us -> none  [the longest x2 8.15 us: mean_rows(): return (total / count[:, None].astype(jnp.float32)).astype(jnp.bfloat16)]
    all_to_all x0 -> x1, blocking collectives: none -> 11.9 us  [shards(): lax.all_to_all(send.reshape(owners, capacity), 'feat', split_axis=0, conc...]
  transfers between devices with their start and end apart: 7 -> 1, of which waited for: 4 -> 0; matrix products, arithmetic and copies ran while one was open for 16% -> 3% of each run, Pallas kernels for 0% -> 50%
where the time goes in v1:
time: 73.7 us; the launch traced here: 73.1 us
  Pallas kernels  50.7 us (69%)
  blocking collectives  11.9 us (16%)
  local copies, waits for them, and re-layouts  4.55 us (6%)
  starting transfers between devices  3.67 us (5%)
  other arithmetic  1.33 us (2%)
  between operations  0.87 us (1%)
    pallas_call x1, Pallas kernels, train(): pl.pallas_call(functools.partial(train_kernel, copies), out_shape=jax.Sha...  18.8 us
    pallas_call x1, Pallas kernels, reduce_grads(): pl.pallas_call(functools.partial(reduce_kernel, owners, trainers, subs, f...  17.8 us
    pallas_call x2, Pallas kernels, take(): pl.pallas_call(take_kernel, out_shape=jax.ShapeDtypeStruct((count, width)...  11.9 us
    all_to_all x1, blocking collectives, shards(): lax.all_to_all(send.reshape(owners, capacity), 'feat', split_axis=0, conc...  11.9 us
    all_to_all x1, starting transfers between devices, shards(): lax.all_to_all(found, 'feat', split_axis=0, concat_axis=0, tiled=True)  3.67 us
    unnamed x30, local copies, waits for them, and re-layouts  2.58 us
    pallas_call x1, Pallas kernels, route(): pl.pallas_call(functools.partial(route_kernel, owners, capacity), out_sha...  2.27 us
  transfers between devices with their start and end apart: 1, of which 0 were waited for; matrix products, arithmetic and copies ran while one was open for 3% of the time, Pallas kernels for 50%

profile of v1, /device:TPU:0, one launch (start us, length us, event | category | flops | bytes accessed | tf_op | source)
XLA Modules:
  0.0 73.1 jit_solution(1381426773999869854)
XLA Ops:
  0.6 1.3 %reduce = s32[2560]{0:T(1024)} reduce(s32[2560,1]{0,1:T(1,128)} %param.26, s32[]{:T(128)} %constant.5.clone.1), dimensions={1}, to_apply=%param.26.reduce_sub_computation | reduce | bytes 20484 | tf_op args[12]
  2.0 2.3 %route.1 = (s32[20,128]{1,0:T(8,128)}, s32[40,128]{1,0:T(8,128)}) custom-call(s32[20,128]{1,0:T(8,128)} %bitcast.23, s32[20,128]{1,0:T(8,128)} %bitcast.25), custom_call_target="tpu_custom_call" | custom-call | tf_op jit(solution)/shard_map/route/pallas_call | solution.py:74
  4.2 11.9 %all_to_all.14 = s32[4,1,1280]{2,1,0:T(1,128)S(1)} all-to-all(s32[4,1,1280]{2,1,0:T(1,128)} %bitcast.24), channel_id=1, replica_groups=mesh['groups'=2,'feat'=4,'trainer'=2,'sub'=2] {'feat'}, dimensions={0} | all-to-all | bytes 40960 | tf_op jit(solution)/shard_map/all_to_all | solution.py:350
  16.2 1.6 %copy-done = bf16[8192,128]{1,0:T(8,128)(2,1)S(1)} copy-done((bf16[8192,128]{1,0:T(8,128)(2,1)S(1)}, bf16[8192,128]{1,0:T(8,128)(2,1)}, u32[]{:S(2)}) %copy-start) | copy-done | bytes 2097176
  17.8 7.6 %take_rows.2 = bf16[5120,128]{1,0:T(8,128)(2,1)} custom-call(s32[5120]{0:T(1024)S(1)} %bitcast.17, bf16[8192,128]{1,0:T(8,128)(2,1)S(1)} %copy-done), custom_call_target="tpu_custom_call" | custom-call | bytes 20971520 | tf_op jit(solution)/shard_map/take_rows/pallas_call | solution.py:103
  25.3 3.7 %all-to-all-start.1 = ((bf16[4,1280,128]{2,1,0:T(8,128)(2,1)}), bf16[4,1280,128]{2,1,0:T(8,128)(2,1)S(1)}, u32[]{:S(2)}, u32[]{:S(2)}) async-start(bf16[4,1280,128]{2,1,0:T(8,128)(2,1)} %bitcast.4), calls=%async_computation.1 | async-start | bytes 2621440 | tf_op jit(solution)/shard_map/all_to_all | solution.py:354
  29.0 0.0 copy-start.12
  29.0 0.0 copy-start.9
  29.1 0.0 copy-start.2
  29.1 0.0 copy-start.3
  29.1 0.0 copy-start.5
  29.1 0.2 copy.30
  29.4 0.3 copy-done.12
  29.7 0.1 copy.31.bias_ref
  29.8 0.1 copy-done.9
  29.9 0.1 copy.32.w2s_ref
  30.0 0.1 copy.33.w2n_ref
  30.1 0.1 copy.34.dlog_ref
  30.3 18.8 %train.1.in_ref = bf16[4,208,256]{2,1,0:T(8,128)(2,1)S(1)} custom-call(bf16[128,2560]{1,0:T(8,128)(2,1)S(1)} %bitcast.16, s32[10,2048]{1,0:T(8,128)S(1)} %bitcast.19, s32[1,2048]{1,0:T(1,128)S(1)} %bitcast.20, s32[5,256]{1,0:T(8,128)S(1)} %bitcast.21, s32[1,256]{1,0:T(1,128)S(1)} %bitcast.22, bf16[128,256]{1,0:T(8,128)(2,1)S(1)} %copy-done.3, ...), custom_call_target="tpu_custom_call" | custom-call | flops 4294967296 | bytes 62914560 | tf_op jit(solution)/shard_map/train/pallas_call | solution.py:226
  49.1 17.8 %reduce_grads.1 = bf16[208,256]{1,0:T(8,128)(2,1)S(1)} custom-call(bf16[4,208,256]{2,1,0:T(8,128)(2,1)S(1)} %train.1.in_ref), custom_call_target="tpu_custom_call" | custom-call | bytes 41943040 | tf_op jit(solution)/shard_map/reduce_grads/pallas_call | solution.py:304
  66.9 0.6 dynamic-slice_bitcast_fusion
  67.5 0.6 fusion.1
  68.1 0.6 fusion
  68.7 4.4 %take_rows.3 = bf16[2560,128]{1,0:T(8,128)(2,1)} custom-call(s32[2560]{0:T(1024)S(1)} %bitcast.18, bf16[5120,128]{1,0:T(8,128)(2,1)S(1)} %bitcast.15), custom_call_target="tpu_custom_call" | custom-call | bytes 20971520 | tf_op jit(solution)/shard_map/take_rows/pallas_call | solution.py:103
  (20 shorter events, 0.1 us)
Async XLA Ops:
  16.2 1.6 %copy-start = (bf16[8192,128]{1,0:T(8,128)(2,1)S(1)}, bf16[8192,128]{1,0:T(8,128)(2,1)}, u32[]{:S(2)}) copy-start(bf16[8192,128]{1,0:T(8,128)(2,1)} %source_ref.1) | copy-start | bytes 6291460
  25.3 3.8 %copy-start.8 = (bf16[2560,128]{1,0:T(8,128)(2,1)S(1)}, bf16[2560,128]{1,0:T(8,128)(2,1)}, u32[]{:S(2)}) copy-start(bf16[2560,128]{1,0:T(8,128)(2,1)} %param.15) | copy-start | bytes 1966084
  25.3 43.4 %all-to-all-start.1 = ((bf16[4,1280,128]{2,1,0:T(8,128)(2,1)}), bf16[4,1280,128]{2,1,0:T(8,128)(2,1)S(1)}, u32[]{:S(2)}, u32[]{:S(2)}) async-start(bf16[4,1280,128]{2,1,0:T(8,128)(2,1)} %bitcast.4), calls=%async_computation.1 | async-start | bytes 2621440 | tf_op jit(solution)/shard_map/all_to_all | solution.py:354
  29.0 0.7 copy-start.12
  29.0 0.9 %copy-start.9 = (bf16[256,172]{0,1:T(8,128)(2,1)S(1)}, bf16[256,172]{0,1:T(8,128)(2,1)}, u32[]{:S(2)}) copy-start(bf16[256,172]{0,1:T(8,128)(2,1)} %param.23) | copy-start | bytes 264196
  29.0 1.0 %copy-start.10 = (bf16[256,172]{0,1:T(8,128)(2,1)S(1)}, bf16[256,172]{0,1:T(8,128)(2,1)}, u32[]{:S(2)}) copy-start(bf16[256,172]{0,1:T(8,128)(2,1)} %param.24) | copy-start | bytes 264196
  29.0 1.1 %copy-start.11 = (bf16[256,172]{0,1:T(8,128)(2,1)S(1)}, bf16[256,172]{0,1:T(8,128)(2,1)}, u32[]{:S(2)}) copy-start(bf16[256,172]{0,1:T(8,128)(2,1)} %param.25) | copy-start | bytes 264196
  29.1 1.2 %copy-start.2 = (s32[2048,10]{0,1:T(8,128)S(1)}, s32[2048,10]{0,1:T(8,128)}, u32[]{:S(2)}) copy-start(s32[2048,10]{0,1:T(8,128)} %param.16) | copy-start | bytes 245764
  29.1 1.2 %copy-start.3 = (bf16[128,256]{1,0:T(8,128)(2,1)S(1)}, bf16[128,256]{1,0:T(8,128)(2,1)}, u32[]{:S(2)}) copy-start(bf16[128,256]{1,0:T(8,128)(2,1)} %w1s_ref.1) | copy-start | bytes 196612
  29.1 1.2 %copy-start.4 = (bf16[128,256]{1,0:T(8,128)(2,1)S(1)}, bf16[128,256]{1,0:T(8,128)(2,1)}, u32[]{:S(2)}) copy-start(bf16[128,256]{1,0:T(8,128)(2,1)} %w1n_ref.1) | copy-start | bytes 196612
  29.1 1.2 %copy-start.5 = (s32[2048]{0:T(1024)S(1)}, s32[2048]{0:T(1024)}, u32[]{:S(2)}) copy-start(s32[2048]{0:T(1024)} %param.17) | copy-start | bytes 24580
  29.1 1.2 %copy-start.6 = (s32[256,5]{0,1:T(8,128)S(1)}, s32[256,5]{0,1:T(8,128)}, u32[]{:S(2)}) copy-start(s32[256,5]{0,1:T(8,128)} %param.18) | copy-start | bytes 15364
  29.1 1.2 %copy-start.7 = (s32[256]{0:T(256)S(1)}, s32[256]{0:T(256)}, u32[]{:S(2)}) copy-start(s32[256]{0:T(256)} %param.19) | copy-start | bytes 3076
  30.3 38.4 %copy-start.1 = (s32[20,128]{1,0:T(8,128)S(1)}, s32[20,128]{1,0:T(8,128)}, u32[]{:S(2)}) copy-start(s32[20,128]{1,0:T(8,128)} %get-tuple-element.8) | copy-start | bytes 30724

commit v2 on v1

v2 whole, which is shorter than its diff:
```python
import functools

import jax
import jax.numpy as jnp
from jax import lax
from jax.experimental import pallas as pl
from jax.experimental.pallas import tpu as pltpu
from jax.sharding import PartitionSpec as P

BF = jnp.bfloat16
F32 = jnp.float32
VM = pl.BlockSpec(memory_space=pltpu.VMEM)
SM = pl.BlockSpec(memory_space=pltpu.SMEM)
MESH = pl.DeviceIdType.MESH
LANES = 128


def mm(left, right):
    return jnp.dot(left, right, preferred_element_type=F32)


def mm_nt(left, right):
    return lax.dot_general(left, right, (((1,), (1,)), ((), ())), preferred_element_type=F32)


def mm_tn(left, right):
    return lax.dot_general(left, right, (((0,), (0,)), ((), ())), preferred_element_type=F32)


def iota(shape, dim):
    return lax.broadcasted_iota(jnp.int32, shape, dim)


def make_requests(owners, capacity, owner_ref, row_ref, slot_ref, send_ref, own_pad):
    rows = owner_ref.shape[0]
    padded = own_pad.shape[0]
    own_pad[...] = jnp.full(own_pad.shape, -1, jnp.int32)
    own_pad[0:rows, :] = owner_ref[...]
    own = own_pad[...]
    before = (iota((LANES, LANES), 0) < iota((LANES, LANES), 1)).astype(F32).astype(BF)
    every = jnp.ones((LANES, LANES), BF)
    above = (iota((padded, padded), 0) > iota((padded, padded), 1)).astype(F32).astype(BF)
    rank = jnp.zeros(own.shape, F32)
    for o in range(owners):
        named = (own == o).astype(F32)
        named16 = named.astype(BF)
        inside = mm(named16, before)
        totals = mm(named16, every).astype(BF)
        rank = rank + named * (inside + mm(above, totals))
    slot = own * capacity + rank.astype(jnp.int32)
    slot = slot[0:rows, :]
    slot_ref[...] = slot
    row = row_ref[...]
    high, low = (row >> 6).astype(F32), (row & 63).astype(F32)
    group, place = slot >> 7, slot & 127
    each = capacity // LANES
    groups = owners * each
    total = jnp.zeros((2 * groups, LANES), F32)
    gid = iota((groups, LANES), 0)
    lid = iota((LANES, LANES), 0)
    for r in range(rows):
        hit = gid == group[r : r + 1, :]
        left = jnp.concatenate(
            [jnp.where(hit, high[r : r + 1, :], 0.0), jnp.where(hit, low[r : r + 1, :], 0.0)], axis=0
        ).astype(BF)
        right = (lid == place[r : r + 1, :]).astype(F32).astype(BF)
        total = total + mm_nt(left, right)
    asked = (total[:groups] * 64.0 + total[groups:]).astype(jnp.int32)
    send_ref[...] = jnp.zeros(send_ref.shape, jnp.int32)
    for o in range(owners):
        send_ref[o, 0:each, :] = asked[o * each : (o + 1) * each]


def step_kernel(
    owners,
    trainers,
    subs,
    capacity,
    factor,
    owner_ref,
    row_ref,
    table_ref,
    feats_t_ref,
    nbr1_ref,
    cnt1_ref,
    nbr2_ref,
    cnt2_ref,
    w1s_ref,
    w1n_ref,
    bias_ref,
    w2s_ref,
    w2n_ref,
    dlog_ref,
    slot_ref,
    replies_ref,
    out_ref,
    own_pad,
    send,
    asked,
    asked_s,
    wide,
    picked,
    found,
    counts1,
    counts2,
    agg_t,
    z_t,
    hid_t,
    packed,
    got,
    part,
    fed,
    load_sem,
    ask_s,
    ask_r,
    rep_s,
    rep_r,
    s1,
    r1,
    s2,
    r2,
):
    copies = trainers * subs
    me = lax.axis_index("trainer") * subs + lax.axis_index("sub")
    feat = lax.axis_index("feat")

    def peer(d):
        p = lax.rem(me + d, copies)
        return p, {"trainer": p // subs, "sub": lax.rem(p, subs)}

    def remote(src, dst, send_sem, recv_sem, where):
        copy = pltpu.make_async_remote_copy(
            src_ref=src,
            dst_ref=dst,
            send_sem=send_sem,
            recv_sem=recv_sem,
            device_id=where,
            device_id_type=MESH,
        )
        copy.start()
        return copy

    barrier = pltpu.get_barrier_semaphore()
    for d in range(1, copies):
        pl.semaphore_signal(barrier, inc=1, device_id=peer(d)[1], device_id_type=MESH)
    for d in range(1, owners):
        pl.semaphore_signal(
            barrier, inc=1, device_id={"feat": lax.rem(feat + d, owners)}, device_id_type=MESH
        )
    make_requests(owners, capacity, owner_ref, row_ref, slot_ref, send, own_pad)
    pl.semaphore_wait(barrier, copies + owners - 2)
    order = sorted(range(1, owners), key=lambda d: abs(2 * d - owners))
    asks = []
    for d in order:
        to = lax.rem(feat + d, owners)
        asks.append(
            remote(send.at[to], asked.at[feat], ask_s.at[d - 1], ask_r.at[d - 1], {"feat": to})
        )
    asked[feat] = send[feat]
    wide[...] = table_ref[...].astype(F32)

    width, front = feats_t_ref.shape
    fan1, mid = nbr1_ref.shape
    fan2, seeds = nbr2_ref.shape
    hidden, classes = w2s_ref.shape
    chunk = seeds
    w1s_t, w1n_t = w1s_ref[...].T, w1n_ref[...].T
    bias = bias_ref[...]
    strip = 32
    one, zero = jnp.ones((strip, chunk), BF), jnp.zeros((strip, chunk), BF)
    base_row = iota((strip, chunk), 0).astype(F32)

    def strips(index_rows, valid_rows, length, put):
        for block in range(0, length, 256):
            rel = []
            for idx, ok in zip(index_rows, valid_rows):
                off = idx - block
                off = jnp.where(ok & (off >= 0) & (off < 256), off, -1).astype(F32)
                rel.append(jnp.broadcast_to(off, (strip, chunk)).astype(BF))
            for s in range(0, min(256, length - block), strip):
                rows = (base_row + float(s)).astype(BF)
                acc = jnp.where(rel[0] == rows, one, zero)
                for r in rel[1:]:
                    acc = acc + jnp.where(r == rows, one, zero)
                put(block + s, acc)

    cnt2 = cnt2_ref[...]

    def put2(at, value):
        counts2[at : at + strip, :] = value

    strips(
        [nbr2_ref[k : k + 1, :] for k in range(fan2)],
        [cnt2 > k for k in range(fan2)],
        mid,
        put2,
    )

    def put1(at, value):
        counts1[at : at + strip, :] = value

    def first_layer(c):
        at = pl.ds(pl.multiple_of(c * chunk, chunk), chunk)
        cnt = cnt1_ref[:, at]
        strips([nbr1_ref[k : k + 1, at] for k in range(fan1)], [cnt > k for k in range(fan1)], front, put1)
        agg = (mm(feats_t_ref[...], counts1[...]) / cnt.astype(F32)).astype(BF)
        agg_t[:, at] = agg
        z = mm(w1s_t, feats_t_ref[:, at]) + mm(w1n_t, agg) + bias
        z_t[:, at] = z
        hid_t[:, at] = (z * jax.nn.sigmoid(z)).astype(BF)

    @pl.loop(0, 1)
    def _(c):
        first_layer(c)

    for copy in asks:
        copy.wait_recv()
    asked[...] = jnp.clip(asked[...], 0, table_ref.shape[0] - 1)
    load = pltpu.make_async_copy(asked, asked_s, load_sem)
    load.start()
    load.wait()

    def gather(to, target):
        @pl.loop(0, capacity // LANES)
        def _(g):
            for j in range(LANES):
                picked[j : j + 1, :] = wide[pl.ds(asked_s[to, g, j], 1), :]
            target[to, pl.ds(pl.multiple_of(g * LANES, LANES), LANES), :] = picked[...].astype(BF)

    answers = []
    for d in order:
        to = lax.rem(feat + d, owners)
        gather(to, found)
        answers.append(
            remote(found.at[to], replies_ref.at[feat], rep_s.at[d - 1], rep_r.at[d - 1], {"feat": to})
        )
    gather(feat, replies_ref)

    @pl.loop(1, mid // chunk)
    def _(c):
        first_layer(c)

    dlog = dlog_ref[...]
    cnt2f = cnt2.astype(F32)
    agg2_t = (mm(hid_t[...], counts2[...]) / cnt2f).astype(BF)
    t2s = mm(hid_t[:, 0:seeds], dlog)
    t2n = mm(agg2_t, dlog)
    dself_t = mm_nt(w2s_ref[...], dlog)
    dneigh_t = mm_nt(w2n_ref[...], dlog) / cnt2f
    dn_high = dneigh_t.astype(BF)
    dn_low = (dneigh_t - dn_high.astype(F32)).astype(BF)
    t1s = jnp.zeros((width, hidden), F32)
    t1n = jnp.zeros((width, hidden), F32)
    tb1 = jnp.zeros((16, hidden), F32)
    ones = jnp.ones((16, chunk), BF)
    for c in range(0, mid, chunk):
        block = counts2[c : c + chunk, :]
        dh = mm_nt(dn_high, block) + mm_nt(dn_low, block)
        if c == 0:
            dh = dh + dself_t
        z = z_t[:, c : c + chunk]
        sig = jax.nn.sigmoid(z)
        dz = (dh * sig * (1.0 + z * (1.0 - sig))).astype(BF)
        t1s = t1s + mm_nt(feats_t_ref[:, c : c + chunk], dz)
        t1n = t1n + mm_nt(agg_t[:, c : c + chunk], dz)
        tb1 = tb1 + mm_nt(ones, dz)
    n1, n2 = width // copies, hidden // copies
    for p in range(copies):
        packed[p, 0:n1, :] = t1s[p * n1 : (p + 1) * n1].astype(BF)
        packed[p, n1 : 2 * n1, :] = t1n[p * n1 : (p + 1) * n1].astype(BF)
        two = 2 * n1
        packed[p, two : two + 2 * n2, :] = jnp.zeros((2 * n2, hidden), BF)
        packed[p, two : two + n2, 0:classes] = t2s[p * n2 : (p + 1) * n2].astype(BF)
        packed[p, two + n2 : two + 2 * n2, 0:classes] = t2n[p * n2 : (p + 1) * n2].astype(BF)
        packed[p, two + 2 * n2 :, :] = jnp.zeros((16, hidden), BF)
        packed[p, two + 2 * n2 :, 0:n2] = tb1[:, p * n2 : (p + 1) * n2].astype(BF)
    first = []
    for d in range(1, copies):
        p, where = peer(d)
        first.append(remote(packed.at[p], got.at[d - 1], s1.at[d - 1], r1.at[d - 1], where))
    total = packed[me].astype(F32)
    for d in range(1, copies):
        first[d - 1].wait_recv()
        total = total + got[d - 1].astype(F32)
    part[...] = total.astype(BF)
    second = []
    for d in order:
        second.append(
            remote(part, fed.at[feat], s2.at[d - 1], r2.at[d - 1], {"feat": lax.rem(feat + d, owners)})
        )
    fed[feat] = part[...]
    for copy in second:
        copy.wait_recv()
    total = fed[0].astype(F32)
    for f in range(1, owners):
        total = total + fed[f].astype(F32)
    out_ref[...] = (total * factor).astype(BF)
    for copy in asks + first + second + answers:
        copy.wait_send()
    for copy in answers:
        copy.wait_recv()


def run_step(owners, trainers, subs, capacity, factor, owner, row, table, feats, nbr1, cnt1, nbr2, cnt2, weights, dlog):
    w1s, w1n, bias, w2s, w2n = weights
    copies = trainers * subs
    front, width = feats.shape
    mid, seeds = nbr1.shape[0], nbr2.shape[0]
    hidden = w1s.shape[1]
    lines = front // LANES
    pages = -(-(capacity // LANES) // 8) * 8
    rows = 2 * width // copies + 2 * hidden // copies + 16
    dma = pltpu.SemaphoreType.DMA
    return pl.pallas_call(
        functools.partial(step_kernel, owners, trainers, subs, capacity, factor),
        out_shape=(
            jax.ShapeDtypeStruct((lines, LANES), jnp.int32),
            jax.ShapeDtypeStruct((owners, capacity, width), BF),
            jax.ShapeDtypeStruct((rows, hidden), BF),
        ),
        in_specs=[VM] * 14,
        out_specs=(VM, VM, VM),
        scratch_shapes=[
            pltpu.VMEM((-(-lines // 16) * 16, LANES), jnp.int32),
            pltpu.VMEM((owners, pages, LANES), jnp.int32),
            pltpu.VMEM((owners, pages, LANES), jnp.int32),
            pltpu.SMEM((owners, pages, LANES), jnp.int32),
            pltpu.VMEM(table.shape, F32),
            pltpu.VMEM((LANES, width), F32),
            pltpu.VMEM((owners, capacity, width), BF),
            pltpu.VMEM((front, seeds), BF),
            pltpu.VMEM((mid, seeds), BF),
            pltpu.VMEM((width, mid), BF),
            pltpu.VMEM((hidden, mid), F32),
            pltpu.VMEM((hidden, mid), BF),
            pltpu.VMEM((copies, rows, hidden), BF),
            pltpu.VMEM((copies - 1, rows, hidden), BF),
            pltpu.VMEM((rows, hidden), BF),
            pltpu.VMEM((owners, rows, hidden), BF),
            dma,
            dma((owners - 1,)),
            dma((owners - 1,)),
            dma((owners - 1,)),
            dma((owners - 1,)),
            dma((copies - 1,)),
            dma((copies - 1,)),
            dma((owners - 1,)),
            dma((owners - 1,)),
        ],
        compiler_params=pltpu.CompilerParams(
            collective_id=0, has_side_effects=True, vmem_limit_bytes=40 << 20
        ),
        cost_estimate=pl.CostEstimate(flops=4 << 30, bytes_accessed=60 << 20, transcendentals=1 << 20),
        name="step",
    )(
        owner.reshape(lines, LANES),
        row.reshape(lines, LANES),
        table,
        feats.T,
        nbr1.T,
        cnt1[None, :],
        nbr2.T,
        cnt2[None, :],
        w1s,
        w1n,
        bias[:, None],
        w2s,
        w2n,
        dlog,
    )


def finish_kernel(slot_ref, source_ref, grads_ref, feats_ref, g1s, g1n, gb, g2s, g2n, wide, picked):
    wide[...] = source_ref[...].astype(F32)

    @pl.loop(0, slot_ref.shape[0])
    def _(g):
        for j in range(LANES):
            picked[j : j + 1, :] = wide[pl.ds(slot_ref[g, j], 1), :]
        feats_ref[pl.ds(pl.multiple_of(g * LANES, LANES), LANES), :] = picked[...].astype(BF)

    n1, n2, classes = g1s.shape[0], g2s.shape[0], g2s.shape[1]
    two = 2 * n1
    g1s[...] = grads_ref[0:n1, :]
    g1n[...] = grads_ref[n1:two, :]
    g2s[...] = grads_ref[two : two + n2, 0:classes]
    g2n[...] = grads_ref[two + n2 : two + 2 * n2, 0:classes]
    gb[...] = grads_ref[two + 2 * n2 : two + 2 * n2 + 1, 0:n2]


def finish(slot, replies, grads, n1, n2, classes):
    count = slot.shape[0] * LANES
    width, hidden = replies.shape[1], grads.shape[1]
    return pl.pallas_call(
        finish_kernel,
        out_shape=(
            jax.ShapeDtypeStruct((count, width), BF),
            jax.ShapeDtypeStruct((n1, hidden), BF),
            jax.ShapeDtypeStruct((n1, hidden), BF),
            jax.ShapeDtypeStruct((1, n2), BF),
            jax.ShapeDtypeStruct((n2, classes), BF),
            jax.ShapeDtypeStruct((n2, classes), BF),
        ),
        in_specs=[SM, VM, VM],
        out_specs=(VM,) * 6,
        scratch_shapes=[pltpu.VMEM(replies.shape, F32), pltpu.VMEM((LANES, width), F32)],
        compiler_params=pltpu.CompilerParams(vmem_limit_bytes=24 << 20),
        name="finish",
    )(slot, replies, grads)


def shards(
    trainers,
    subs,
    owners,
    table,
    cur_feats,
    nbr_first,
    cnt_first,
    nbr_second,
    cnt_second,
    w1_self,
    w1_neigh,
    bias_first,
    w2_self,
    w2_neigh,
    dlogits,
    next_owner,
    next_row,
):
    copies = trainers * subs
    front_rows, width = cur_feats.shape
    hidden, classes = w2_self.shape
    capacity = -(-(2 * front_rows // owners) // LANES) * LANES
    seeds_all = nbr_second.shape[0] * owners * copies
    slot, replies, grads = run_step(
        owners,
        trainers,
        subs,
        capacity,
        float(seeds_all) ** -0.5,
        next_owner[:, 0],
        next_row,
        table,
        cur_feats,
        nbr_first,
        cnt_first,
        nbr_second,
        cnt_second,
        (w1_self, w1_neigh, bias_first, w2_self, w2_neigh),
        dlogits,
    )
    n1, n2 = width // copies, hidden // copies
    feats, g1s, g1n, gb, g2s, g2n = finish(
        slot, replies.reshape(-1, width), grads, n1, n2, classes
    )
    return feats, g1s, g1n, gb.reshape(-1), g2s, g2n


def solution(mesh):
    every = ("groups", "feat", "trainer", "sub")
    share = ("groups", "trainer", "sub")
    placed = (
        P(("groups", "feat"), None),
        P(every, None),
        P(every, None),
        P(every),
        P(every, None),
        P(every),
        P("groups", None),
        P("groups", None),
        P("groups"),
        P("groups", None),
        P("groups", None),
        P(every, None),
        P(every, None),
        P(every),
    )
    shape = mesh.shape
    return jax.shard_map(
        functools.partial(shards, shape["trainer"], shape["sub"], shape["feat"]),
        mesh=mesh,
        in_specs=placed,
        out_specs=(
            P(every, None),
            P(share, None),
            P(share, None),
            P(share),
            P(share, None),
            P(share, None),
        ),
        check_vma=False,
    )
```

time: 73.7 us -> 61.8 us (0.84)
  blocking collectives: 11.9 us -> 0 us
  starting transfers between devices: 3.67 us -> 0 us
  local copies, waits for them, and re-layouts: 4.55 us -> 7.7 us
  Pallas kernels: 50.7 us -> 52 us
    all_to_all x1 -> x0, blocking collectives: 11.9 us -> none  [shards(): lax.all_to_all(send.reshape(owners, capacity), 'feat', split_axis=0, conc...]
    unnamed x30 -> x20, local copies, waits for them, and re-layouts: 2.58 us -> 6.9 us
    all_to_all x1 -> x0, starting transfers between devices: 3.67 us -> none  [shards(): lax.all_to_all(found, 'feat', split_axis=0, concat_axis=0, tiled=True)]
    pallas_call x5 -> x2, Pallas kernels: 50.7 us -> 52 us  [the longest x1 47.8 us: run_step(): pl.pallas_call(functools.partial(step_kernel, owners, trainers, subs, cap...]
    slice x3 -> x0, local copies, waits for them, and re-layouts: 1.25 us -> none  [the longest x1 0.63 us: shards(): summed[two + r2:two + 2 * r2, 0:classes]]
  transfers between devices with their start and end apart: 1 -> 0, of which waited for: 0 -> 0; matrix products, arithmetic and copies ran while one was open for 3% -> 0% of each run, Pallas kernels for 50% -> 0%
where the time goes in v2:
time: 61.8 us; the launch traced here: 61.4 us
  Pallas kernels  52 us (84%)
  local copies, waits for them, and re-layouts  7.7 us (12%)
  other arithmetic  0.88 us (1%)
  between operations  0.77 us (1%)
    pallas_call x1, Pallas kernels, run_step(): pl.pallas_call(functools.partial(step_kernel, owners, trainers, subs, cap...  47.8 us
    unnamed x20, local copies, waits for them, and re-layouts  6.9 us
    pallas_call x1, Pallas kernels, finish(): pl.pallas_call(finish_kernel, out_shape=(jax.ShapeDtypeStruct((count, wid...  4.17 us

profile of v2, /device:TPU:0, one launch (start us, length us, event | category | flops | bytes accessed | tf_op | source)
XLA Modules:
  0.0 61.4 jit_solution(15658813801470267182)
XLA Ops:
  0.6 0.0 copy-start.4
  0.6 0.0 copy-start.7
  0.7 0.0 copy-start.6
  0.7 0.0 copy-start.5
  0.7 0.0 copy-start
  0.7 0.9 %reduce = s32[2560]{0:T(1024)S(1)} reduce(s32[2560,1]{0,1:T(1,128)} %param.26, s32[]{:T(128)} %constant), dimensions={1}, to_apply=%param.26.reduce_sub_computation | reduce | bytes 20484 | tf_op args[12]
  1.6 0.8 %copy.25.bias_ref = f32[256,1]{1,0:T(8,128)S(1)} copy(f32[256,1]{0,1:T(1,128)} %bitcast.18) | data formatting | bytes 2048 | tf_op jit(solution)/shard_map/broadcast_in_dim | solution.py:366
  2.4 1.0 %copy.26.w2s_ref = bf16[256,172]{1,0:T(8,128)(2,1)S(1)} copy(bf16[256,172]{0,1:T(8,128)(2,1)} %param.23) | data formatting | bytes 176128 | tf_op args[9]
  3.4 1.0 %copy.27.w2n_ref = bf16[256,172]{1,0:T(8,128)(2,1)S(1)} copy(bf16[256,172]{0,1:T(8,128)(2,1)} %param.24) | data formatting | bytes 176128 | tf_op args[10]
  4.4 1.0 %copy.28.dlog_ref = bf16[256,172]{1,0:T(8,128)(2,1)S(1)} copy(bf16[256,172]{0,1:T(8,128)(2,1)} %param.25) | data formatting | bytes 176128 | tf_op args[11]
  5.4 1.3 %copy.24 = bf16[2560,128]{0,1:T(8,128)(2,1)S(1)} copy(bf16[2560,128]{1,0:T(8,128)(2,1)} %param.15) | data formatting | bytes 1310720 | tf_op args[1]
  6.7 0.0 copy-done.4
  6.7 0.0 copy-done.7
  6.7 0.0 copy-done.6
  6.7 0.0 copy-done.5
  6.8 0.0 copy-done
  6.8 0.0 copy-start.1
  6.8 0.9 %copy-done.1 = s32[2048,10]{0,1:T(8,128)S(1)} copy-done((s32[2048,10]{0,1:T(8,128)S(1)}, s32[2048,10]{0,1:T(8,128)}, u32[]{:S(2)}) %copy-start.1) | copy-done | bytes 81944
  7.7 0.0 copy-start.2
  7.7 0.8 %copy-done.2 = bf16[128,256]{1,0:T(8,128)(2,1)S(1)} copy-done((bf16[128,256]{1,0:T(8,128)(2,1)S(1)}, bf16[128,256]{1,0:T(8,128)(2,1)}, u32[]{:S(2)}) %copy-start.2) | copy-done | bytes 65560
  8.5 0.0 copy-start.3
  8.5 0.8 %copy-done.3 = bf16[128,256]{1,0:T(8,128)(2,1)S(1)} copy-done((bf16[128,256]{1,0:T(8,128)(2,1)S(1)}, bf16[128,256]{1,0:T(8,128)(2,1)}, u32[]{:S(2)}) %copy-start.3) | copy-done | bytes 65560
  9.3 47.8 %step.1 = (s32[20,128]{1,0:T(8,128)S(1)}, bf16[4,1280,128]{2,1,0:T(8,128)(2,1)S(1)}, bf16[208,256]{1,0:T(8,128)(2,1)S(1)}) custom-call(s32[20,128]{1,0:T(8,128)S(1)} %bitcast.12, s32[20,128]{1,0:T(8,128)S(1)} %bitcast.14, bf16[8192,128]{1,0:T(8,128)(2,1)S(1)} %copy-done, bf16[128,2560]{1,0:T(8,128)(2,1)S(1)} %bitcast.11, s32[10,2048]{1,0:T(8,128)S(1)} %bitcast.13, ...), custom_call_target="tpu_custom_call" | custom-call | flops 4294967296 | bytes 62914560 | tf_op jit(solution)/shard_map/step/pallas_call | solution.py:314
  57.2 4.2 %finish.1 = (bf16[2560,128]{1,0:T(8,128)(2,1)}, bf16[32,256]{1,0:T(8,128)(2,1)}, bf16[32,256]{1,0:T(8,128)(2,1)}, bf16[1,64]{1,0:T(2,128)(2,1)}, bf16[64,172]{1,0:T(8,128)(2,1)}, /*index=5*/bf16[64,172]{1,0:T(8,128)(2,1)}) custom-call(s32[20,128]{1,0:T(8,128)S(1)} %get-tuple-element.15.slot_ref, bf16[5120,128]{1,0:T(8,128)(2,1)S(1)} %bitcast.10, ...), custom_call_target="tpu_custom_call" | custom-call | tf_op jit(solution)/shard_map/finish/pallas_call | solution.py:394
Async XLA Ops:
  0.6 6.1 %copy-start.4 = (s32[2560]{0:T(1024)S(1)}, s32[2560]{0:T(1024)}, u32[]{:S(2)}) copy-start(s32[2560]{0:T(1024)} %param.27) | copy-start | bytes 30724
  0.6 6.1 %copy-start.7 = (s32[256]{0:T(256)S(1)}, s32[256]{0:T(256)}, u32[]{:S(2)}) copy-start(s32[256]{0:T(256)} %param.19) | copy-start | bytes 3076
  0.7 6.1 %copy-start.6 = (s32[256,5]{0,1:T(8,128)S(1)}, s32[256,5]{0,1:T(8,128)}, u32[]{:S(2)}) copy-start(s32[256,5]{0,1:T(8,128)} %param.18) | copy-start | bytes 15364
  0.7 6.1 %copy-start.5 = (s32[2048]{0:T(1024)S(1)}, s32[2048]{0:T(1024)}, u32[]{:S(2)}) copy-start(s32[2048]{0:T(1024)} %param.17) | copy-start | bytes 24580
  0.7 6.1 %copy-start = (bf16[8192,128]{1,0:T(8,128)(2,1)S(1)}, bf16[8192,128]{1,0:T(8,128)(2,1)}, u32[]{:S(2)}) copy-start(bf16[8192,128]{1,0:T(8,128)(2,1)} %table_ref.1) | copy-start | bytes 6291460
  6.8 0.9 %copy-start.1 = (s32[2048,10]{0,1:T(8,128)S(1)}, s32[2048,10]{0,1:T(8,128)}, u32[]{:S(2)}) copy-start(s32[2048,10]{0,1:T(8,128)} %param.16) | copy-start | bytes 245764
  7.7 0.8 %copy-start.2 = (bf16[128,256]{1,0:T(8,128)(2,1)S(1)}, bf16[128,256]{1,0:T(8,128)(2,1)}, u32[]{:S(2)}) copy-start(bf16[128,256]{1,0:T(8,128)(2,1)} %w1s_ref.1) | copy-start | bytes 196612
  8.5 0.8 %copy-start.3 = (bf16[128,256]{1,0:T(8,128)(2,1)S(1)}, bf16[128,256]{1,0:T(8,128)(2,1)}, u32[]{:S(2)}) copy-start(bf16[128,256]{1,0:T(8,128)(2,1)} %w1n_ref.1) | copy-start | bytes 196612

commit v3 on v2

--- a/solution.py
+++ b/solution.py
@@ -10,6 +10,7 @@
 BF = jnp.bfloat16
 F32 = jnp.float32
 VM = pl.BlockSpec(memory_space=pltpu.VMEM)
+AN = pl.BlockSpec(memory_space=pl.ANY)
 SM = pl.BlockSpec(memory_space=pltpu.SMEM)
 MESH = pl.DeviceIdType.MESH
 LANES = 128
@@ -32,10 +33,11 @@
 
 
 def make_requests(owners, capacity, owner_ref, row_ref, slot_ref, send_ref, own_pad):
-    rows = owner_ref.shape[0]
+    rows = row_ref.shape[0]
     padded = own_pad.shape[0]
     own_pad[...] = jnp.full(own_pad.shape, -1, jnp.int32)
-    own_pad[0:rows, :] = owner_ref[...]
+    for r in range(rows):
+        own_pad[r : r + 1, :] = owner_ref[:, r * LANES : (r + 1) * LANES]
     own = own_pad[...]
     before = (iota((LANES, LANES), 0) < iota((LANES, LANES), 1)).astype(F32).astype(BF)
     every = jnp.ones((LANES, LANES), BF)
@@ -79,14 +81,14 @@
     factor,
     owner_ref,
     row_ref,
-    table_ref,
-    feats_t_ref,
-    nbr1_ref,
+    table_h,
+    feats_h,
+    nbr1_h,
     cnt1_ref,
     nbr2_ref,
     cnt2_ref,
-    w1s_ref,
-    w1n_ref,
+    w1s_h,
+    w1n_h,
     bias_ref,
     w2s_ref,
     w2n_ref,
@@ -94,6 +96,13 @@
     slot_ref,
     replies_ref,
     out_ref,
+    table_ref,
+    feats_v,
+    feats_t_ref,
+    nbr1_ref,
+    w1s_ref,
+    w1n_ref,
+    fetch_sem,
     own_pad,
     send,
     asked,
@@ -140,6 +149,18 @@
         copy.start()
         return copy
 
+    fetches = []
+    for n, (src, dst) in enumerate(
+        (
+            (table_h, table_ref),
+            (feats_h, feats_v),
+            (nbr1_h, nbr1_ref),
+            (w1s_h, w1s_ref),
+            (w1n_h, w1n_ref),
+        )
+    ):
+        fetches.append(pltpu.make_async_copy(src, dst, fetch_sem.at[n]))
+        fetches[-1].start()
     barrier = pltpu.get_barrier_semaphore()
     for d in range(1, copies):
         pl.semaphore_signal(barrier, inc=1, device_id=peer(d)[1], device_id_type=MESH)
@@ -157,15 +178,19 @@
             remote(send.at[to], asked.at[feat], ask_s.at[d - 1], ask_r.at[d - 1], {"feat": to})
         )
     asked[feat] = send[feat]
+    for fetch in fetches:
+        fetch.wait()
     wide[...] = table_ref[...].astype(F32)
+    for r in range(0, feats_v.shape[0], LANES):
+        feats_t_ref[:, r : r + LANES] = feats_v[r : r + LANES, :].T
 
     width, front = feats_t_ref.shape
     fan1, mid = nbr1_ref.shape
     fan2, seeds = nbr2_ref.shape
-    hidden, classes = w2s_ref.shape
+    classes, hidden = w2s_ref.shape
     chunk = seeds
     w1s_t, w1n_t = w1s_ref[...].T, w1n_ref[...].T
-    bias = bias_ref[...]
+    bias = jnp.broadcast_to(bias_ref[...], (LANES, hidden)).T[:, 0:1]
     strip = 32
     one, zero = jnp.ones((strip, chunk), BF), jnp.zeros((strip, chunk), BF)
     base_row = iota((strip, chunk), 0).astype(F32)
@@ -243,10 +268,10 @@
     dlog = dlog_ref[...]
     cnt2f = cnt2.astype(F32)
     agg2_t = (mm(hid_t[...], counts2[...]) / cnt2f).astype(BF)
-    t2s = mm(hid_t[:, 0:seeds], dlog)
-    t2n = mm(agg2_t, dlog)
-    dself_t = mm_nt(w2s_ref[...], dlog)
-    dneigh_t = mm_nt(w2n_ref[...], dlog) / cnt2f
+    t2s = mm_nt(hid_t[:, 0:seeds], dlog)
+    t2n = mm_nt(agg2_t, dlog)
+    dself_t = mm_tn(w2s_ref[...], dlog)
+    dneigh_t = mm_tn(w2n_ref[...], dlog) / cnt2f
     dn_high = dneigh_t.astype(BF)
     dn_low = (dneigh_t - dn_high.astype(F32)).astype(BF)
     t1s = jnp.zeros((width, hidden), F32)
@@ -318,9 +343,16 @@
             jax.ShapeDtypeStruct((owners, capacity, width), BF),
             jax.ShapeDtypeStruct((rows, hidden), BF),
         ),
-        in_specs=[VM] * 14,
+        in_specs=[VM, VM, AN, AN, AN, VM, VM, VM, AN, AN, VM, VM, VM, VM],
         out_specs=(VM, VM, VM),
         scratch_shapes=[
+            pltpu.VMEM(table.shape, BF),
+            pltpu.VMEM(feats.shape, BF),
+            pltpu.VMEM((width, front), BF),
+            pltpu.VMEM((nbr1.shape[1], mid), jnp.int32),
+            pltpu.VMEM(w1s.shape, BF),
+            pltpu.VMEM(w1n.shape, BF),
+            dma((5,)),
             pltpu.VMEM((-(-lines // 16) * 16, LANES), jnp.int32),
             pltpu.VMEM((owners, pages, LANES), jnp.int32),
             pltpu.VMEM((owners, pages, LANES), jnp.int32),
@@ -353,20 +385,20 @@
         cost_estimate=pl.CostEstimate(flops=4 << 30, bytes_accessed=60 << 20, transcendentals=1 << 20),
         name="step",
     )(
-        owner.reshape(lines, LANES),
+        owner.T,
         row.reshape(lines, LANES),
         table,
-        feats.T,
+        feats,
         nbr1.T,
         cnt1[None, :],
         nbr2.T,
         cnt2[None, :],
         w1s,
         w1n,
-        bias[:, None],
-        w2s,
-        w2n,
-        dlog,
+        bias[None, :],
+        w2s.T,
+        w2n.T,
+        dlog.T,
     )
 
 
@@ -439,7 +471,7 @@
         subs,
         capacity,
         float(seeds_all) ** -0.5,
-        next_owner[:, 0],
+        next_owner,
         next_row,
         table,
         cur_feats,

time: 61.8 us -> 66.2 us (1.071)
  local copies, waits for them, and re-layouts: 7.7 us -> 12.1 us
  Pallas kernels: 52 us -> 52.9 us
  other arithmetic: 0.88 us -> 0 us
    unnamed x20 -> x28, local copies, waits for them, and re-layouts: 6.9 us -> 12.1 us
    unnamed x1 -> x0, other arithmetic: 0.88 us -> none
    pallas_call x1, Pallas kernels: 47.8 us -> 48.7 us  [run_step(): pl.pallas_call(functools.partial(step_kernel, owners, trainers, subs, cap...]
    broadcast_in_dim x1 -> x0, local copies, waits for them, and re-layouts: 0.81 us -> none  [run_step(): bias[:, None]]
where the time goes in v3:
time: 66.2 us; the launch traced here: 65.6 us
  Pallas kernels  52.9 us (80%)
  local copies, waits for them, and re-layouts  12.1 us (18%)
  between operations  0.67 us (1%)
    pallas_call x1, Pallas kernels, run_step(): pl.pallas_call(functools.partial(step_kernel, owners, trainers, subs, cap...  48.7 us
    unnamed x28, local copies, waits for them, and re-layouts  12.1 us
    pallas_call x1, Pallas kernels, finish(): pl.pallas_call(finish_kernel, out_shape=(jax.ShapeDtypeStruct((count, wid...  4.17 us

profile of v3, /device:TPU:0, one launch (start us, length us, event | category | flops | bytes accessed | tf_op | source)
XLA Modules:
  0.0 65.6 jit_solution(1395986644631561149)
XLA Ops:
  0.6 0.0 copy-start
  0.6 1.6 %copy-done = bf16[8192,128]{1,0:T(8,128)(2,1)S(1)} copy-done((bf16[8192,128]{1,0:T(8,128)(2,1)S(1)}, bf16[8192,128]{1,0:T(8,128)(2,1)}, u32[]{:S(2)}) %copy-start) | copy-done | bytes 2097176
  2.2 0.0 copy-start.1
  2.2 1.1 %copy-done.1 = bf16[2560,128]{1,0:T(8,128)(2,1)S(1)} copy-done((bf16[2560,128]{1,0:T(8,128)(2,1)S(1)}, bf16[2560,128]{1,0:T(8,128)(2,1)}, u32[]{:S(2)}) %copy-start.1) | copy-done | bytes 655384
  3.3 0.0 copy-start.2
  3.3 0.9 %copy-done.2 = s32[2048,10]{0,1:T(8,128)S(1)} copy-done((s32[2048,10]{0,1:T(8,128)S(1)}, s32[2048,10]{0,1:T(8,128)}, u32[]{:S(2)}) %copy-start.2) | copy-done | bytes 81944
  4.2 0.9 %copy-done.3 = bf16[256,172]{0,1:T(8,128)(2,1)S(1)} copy-done((bf16[256,172]{0,1:T(8,128)(2,1)S(1)}, bf16[256,172]{0,1:T(8,128)(2,1)}, u32[]{:S(2)}) %copy-start.3) | copy-done | bytes 88088
  5.1 0.0 copy-start.4
  5.1 0.9 %copy-done.4 = bf16[256,172]{0,1:T(8,128)(2,1)S(1)} copy-done((bf16[256,172]{0,1:T(8,128)(2,1)S(1)}, bf16[256,172]{0,1:T(8,128)(2,1)}, u32[]{:S(2)}) %copy-start.4) | copy-done | bytes 88088
  6.0 0.0 copy-start.5
  6.0 0.9 %copy-done.5 = bf16[256,172]{0,1:T(8,128)(2,1)S(1)} copy-done((bf16[256,172]{0,1:T(8,128)(2,1)S(1)}, bf16[256,172]{0,1:T(8,128)(2,1)}, u32[]{:S(2)}) %copy-start.5) | copy-done | bytes 88088
  6.9 0.0 copy-start.6
  6.9 0.8 %copy-done.6 = bf16[128,256]{1,0:T(8,128)(2,1)S(1)} copy-done((bf16[128,256]{1,0:T(8,128)(2,1)S(1)}, bf16[128,256]{1,0:T(8,128)(2,1)}, u32[]{:S(2)}) %copy-start.6) | copy-done | bytes 65560
  7.7 0.0 copy-start.7
  7.7 0.8 %copy-done.7 = bf16[128,256]{1,0:T(8,128)(2,1)S(1)} copy-done((bf16[128,256]{1,0:T(8,128)(2,1)S(1)}, bf16[128,256]{1,0:T(8,128)(2,1)}, u32[]{:S(2)}) %copy-start.7) | copy-done | bytes 65560
  8.6 0.0 copy-start.8
  8.6 0.7 %copy-done.8 = s32[2560]{0:T(1024)S(1)} copy-done((s32[2560]{0:T(1024)S(1)}, s32[2560]{0:T(1024)}, u32[]{:S(2)}) %copy-start.8) | copy-done | bytes 10264
  9.3 0.7 %copy-done.9 = s32[2560,1]{0,1:T(1,128)S(1)} copy-done((s32[2560,1]{0,1:T(1,128)S(1)}, s32[2560,1]{0,1:T(1,128)}, u32[]{:S(2)}) %copy-start.9) | copy-done | bytes 10264
  10.0 0.7 %copy-done.10 = s32[2048]{0:T(1024)S(1)} copy-done((s32[2048]{0:T(1024)S(1)}, s32[2048]{0:T(1024)}, u32[]{:S(2)}) %copy-start.10) | copy-done | bytes 8216
  10.7 0.7 %copy-done.11 = s32[256,5]{0,1:T(8,128)S(1)} copy-done((s32[256,5]{0,1:T(8,128)S(1)}, s32[256,5]{0,1:T(8,128)}, u32[]{:S(2)}) %copy-start.11) | copy-done | bytes 5144
  11.4 0.7 %copy-done.12 = s32[256]{0:T(256)S(1)} copy-done((s32[256]{0:T(256)S(1)}, s32[256]{0:T(256)}, u32[]{:S(2)}) %copy-start.12) | copy-done | bytes 1048
  12.1 0.7 %copy-done.13 = f32[256]{0:T(256)S(1)} copy-done((f32[256]{0:T(256)S(1)}, f32[256]{0:T(256)}, u32[]{:S(2)}) %copy-start.13) | copy-done | bytes 1048
  12.7 48.7 %step.1 = (s32[20,128]{1,0:T(8,128)S(1)}, bf16[4,1280,128]{2,1,0:T(8,128)(2,1)S(1)}, bf16[208,256]{1,0:T(8,128)(2,1)S(1)}) custom-call(s32[1,2560]{1,0:T(1,128)S(1)} %bitcast.18, s32[20,128]{1,0:T(8,128)S(1)} %bitcast.17, bf16[8192,128]{1,0:T(8,128)(2,1)S(1)} %copy-done, bf16[2560,128]{1,0:T(8,128)(2,1)S(1)} %copy-done.1, s32[10,2048]{1,0:T(8,128)S(1)} %bitcast.13, ...), custom_call_target="tpu_custom_call" | custom-call | flops 4294967296 | bytes 62914560 | tf_op jit(solution)/shard_map/step/pallas_call | solution.py:339
  61.4 4.2 %finish.1 = (bf16[2560,128]{1,0:T(8,128)(2,1)}, bf16[32,256]{1,0:T(8,128)(2,1)}, bf16[32,256]{1,0:T(8,128)(2,1)}, bf16[1,64]{1,0:T(2,128)(2,1)}, bf16[64,172]{1,0:T(8,128)(2,1)}, /*index=5*/bf16[64,172]{1,0:T(8,128)(2,1)}) custom-call(s32[20,128]{1,0:T(8,128)S(1)} %get-tuple-element.15.slot_ref, bf16[5120,128]{1,0:T(8,128)(2,1)S(1)} %bitcast.12, ...), custom_call_target="tpu_custom_call" | custom-call | tf_op jit(solution)/shard_map/finish/pallas_call | solution.py:426
  (6 shorter events, 0.0 us)
Async XLA Ops:
  0.6 1.6 %copy-start = (bf16[8192,128]{1,0:T(8,128)(2,1)S(1)}, bf16[8192,128]{1,0:T(8,128)(2,1)}, u32[]{:S(2)}) copy-start(bf16[8192,128]{1,0:T(8,128)(2,1)} %table_h.1) | copy-start | bytes 6291460
  2.2 1.1 %copy-start.1 = (bf16[2560,128]{1,0:T(8,128)(2,1)S(1)}, bf16[2560,128]{1,0:T(8,128)(2,1)}, u32[]{:S(2)}) copy-start(bf16[2560,128]{1,0:T(8,128)(2,1)} %feats_h.1) | copy-start | bytes 1966084
  3.3 0.9 %copy-start.2 = (s32[2048,10]{0,1:T(8,128)S(1)}, s32[2048,10]{0,1:T(8,128)}, u32[]{:S(2)}) copy-start(s32[2048,10]{0,1:T(8,128)} %param.16) | copy-start | bytes 245764
  4.2 0.9 %copy-start.3 = (bf16[256,172]{0,1:T(8,128)(2,1)S(1)}, bf16[256,172]{0,1:T(8,128)(2,1)}, u32[]{:S(2)}) copy-start(bf16[256,172]{0,1:T(8,128)(2,1)} %param.23) | copy-start | bytes 264196
  5.1 0.9 %copy-start.4 = (bf16[256,172]{0,1:T(8,128)(2,1)S(1)}, bf16[256,172]{0,1:T(8,128)(2,1)}, u32[]{:S(2)}) copy-start(bf16[256,172]{0,1:T(8,128)(2,1)} %param.24) | copy-start | bytes 264196
  6.0 0.9 %copy-start.5 = (bf16[256,172]{0,1:T(8,128)(2,1)S(1)}, bf16[256,172]{0,1:T(8,128)(2,1)}, u32[]{:S(2)}) copy-start(bf16[256,172]{0,1:T(8,128)(2,1)} %param.25) | copy-start | bytes 264196
  6.9 0.8 %copy-start.6 = (bf16[128,256]{1,0:T(8,128)(2,1)S(1)}, bf16[128,256]{1,0:T(8,128)(2,1)}, u32[]{:S(2)}) copy-start(bf16[128,256]{1,0:T(8,128)(2,1)} %w1s_h.1) | copy-start | bytes 196612
  7.7 0.8 %copy-start.7 = (bf16[128,256]{1,0:T(8,128)(2,1)S(1)}, bf16[128,256]{1,0:T(8,128)(2,1)}, u32[]{:S(2)}) copy-start(bf16[128,256]{1,0:T(8,128)(2,1)} %w1n_h.1) | copy-start | bytes 196612
  8.6 0.7 %copy-start.8 = (s32[2560]{0:T(1024)S(1)}, s32[2560]{0:T(1024)}, u32[]{:S(2)}) copy-start(s32[2560]{0:T(1024)} %param.27) | copy-start | bytes 30724
  9.3 0.7 %copy-start.9 = (s32[2560,1]{0,1:T(1,128)S(1)}, s32[2560,1]{0,1:T(1,128)}, u32[]{:S(2)}) copy-start(s32[2560,1]{0,1:T(1,128)} %param.26) | copy-start | bytes 30724
  10.0 0.7 %copy-start.10 = (s32[2048]{0:T(1024)S(1)}, s32[2048]{0:T(1024)}, u32[]{:S(2)}) copy-start(s32[2048]{0:T(1024)} %param.17) | copy-start | bytes 24580
  10.7 0.7 %copy-start.11 = (s32[256,5]{0,1:T(8,128)S(1)}, s32[256,5]{0,1:T(8,128)}, u32[]{:S(2)}) copy-start(s32[256,5]{0,1:T(8,128)} %param.18) | copy-start | bytes 15364
  11.4 0.7 %copy-start.12 = (s32[256]{0:T(256)S(1)}, s32[256]{0:T(256)}, u32[]{:S(2)}) copy-start(s32[256]{0:T(256)} %param.19) | copy-start | bytes 3076
  12.1 0.7 %copy-start.13 = (f32[256]{0:T(256)S(1)}, f32[256]{0:T(256)}, u32[]{:S(2)}) copy-start(f32[256]{0:T(256)} %param.22) | copy-start | bytes 3076

commit v4 on v3

--- a/solution.py
+++ b/solution.py
@@ -10,7 +10,7 @@
 BF = jnp.bfloat16
 F32 = jnp.float32
 VM = pl.BlockSpec(memory_space=pltpu.VMEM)
-AN = pl.BlockSpec(memory_space=pl.ANY)
+HB = pl.BlockSpec(memory_space=pltpu.HBM)
 SM = pl.BlockSpec(memory_space=pltpu.SMEM)
 MESH = pl.DeviceIdType.MESH
 LANES = 128
@@ -79,17 +79,17 @@
     subs,
     capacity,
     factor,
-    owner_ref,
-    row_ref,
+    owner_h,
+    row_h,
     table_h,
     feats_h,
     nbr1_h,
-    cnt1_ref,
-    nbr2_ref,
-    cnt2_ref,
+    cnt1_h,
+    nbr2_h,
+    cnt2_h,
     w1s_h,
     w1n_h,
-    bias_ref,
+    bias_h,
     w2s_ref,
     w2n_ref,
     dlog_ref,
@@ -102,6 +102,12 @@
     nbr1_ref,
     w1s_ref,
     w1n_ref,
+    owner_ref,
+    row_ref,
+    cnt1_ref,
+    nbr2_ref,
+    cnt2_ref,
+    bias_ref,
     fetch_sem,
     own_pad,
     send,
@@ -152,11 +158,17 @@
     fetches = []
     for n, (src, dst) in enumerate(
         (
+            (owner_h, owner_ref),
+            (row_h, row_ref),
             (table_h, table_ref),
             (feats_h, feats_v),
             (nbr1_h, nbr1_ref),
             (w1s_h, w1s_ref),
             (w1n_h, w1n_ref),
+            (cnt1_h, cnt1_ref),
+            (nbr2_h, nbr2_ref),
+            (cnt2_h, cnt2_ref),
+            (bias_h, bias_ref),
         )
     ):
         fetches.append(pltpu.make_async_copy(src, dst, fetch_sem.at[n]))
@@ -168,6 +180,8 @@
         pl.semaphore_signal(
             barrier, inc=1, device_id={"feat": lax.rem(feat + d, owners)}, device_id_type=MESH
         )
+    fetches[0].wait()
+    fetches[1].wait()
     make_requests(owners, capacity, owner_ref, row_ref, slot_ref, send, own_pad)
     pl.semaphore_wait(barrier, copies + owners - 2)
     order = sorted(range(1, owners), key=lambda d: abs(2 * d - owners))
@@ -178,7 +192,7 @@
             remote(send.at[to], asked.at[feat], ask_s.at[d - 1], ask_r.at[d - 1], {"feat": to})
         )
     asked[feat] = send[feat]
-    for fetch in fetches:
+    for fetch in fetches[2:]:
         fetch.wait()
     wide[...] = table_ref[...].astype(F32)
     for r in range(0, feats_v.shape[0], LANES):
@@ -343,7 +357,7 @@
             jax.ShapeDtypeStruct((owners, capacity, width), BF),
             jax.ShapeDtypeStruct((rows, hidden), BF),
         ),
-        in_specs=[VM, VM, AN, AN, AN, VM, VM, VM, AN, AN, VM, VM, VM, VM],
+        in_specs=[HB] * 11 + [VM] * 3,
         out_specs=(VM, VM, VM),
         scratch_shapes=[
             pltpu.VMEM(table.shape, BF),
@@ -352,7 +366,13 @@
             pltpu.VMEM((nbr1.shape[1], mid), jnp.int32),
             pltpu.VMEM(w1s.shape, BF),
             pltpu.VMEM(w1n.shape, BF),
-            dma((5,)),
+            pltpu.VMEM((1, front), jnp.int32),
+            pltpu.VMEM((lines, LANES), jnp.int32),
+            pltpu.VMEM((1, mid), jnp.int32),
+            pltpu.VMEM((nbr2.shape[1], seeds), jnp.int32),
+            pltpu.VMEM((1, seeds), jnp.int32),
+            pltpu.VMEM((1, hidden), F32),
+            dma((11,)),
             pltpu.VMEM((-(-lines // 16) * 16, LANES), jnp.int32),
             pltpu.VMEM((owners, pages, LANES), jnp.int32),
             pltpu.VMEM((owners, pages, LANES), jnp.int32),
@@ -380,7 +400,7 @@
             dma((owners - 1,)),
         ],
         compiler_params=pltpu.CompilerParams(
-            collective_id=0, has_side_effects=True, vmem_limit_bytes=40 << 20
+            collective_id=0, has_side_effects=True, vmem_limit_bytes=61 << 20
         ),
         cost_estimate=pl.CostEstimate(flops=4 << 30, bytes_accessed=60 << 20, transcendentals=1 << 20),
         name="step",
@@ -436,7 +456,7 @@
         in_specs=[SM, VM, VM],
         out_specs=(VM,) * 6,
         scratch_shapes=[pltpu.VMEM(replies.shape, F32), pltpu.VMEM((LANES, width), F32)],
-        compiler_params=pltpu.CompilerParams(vmem_limit_bytes=24 << 20),
+        compiler_params=pltpu.CompilerParams(vmem_limit_bytes=61 << 20),
         name="finish",
     )(slot, replies, grads)
 

time: 66.2 us -> 55.9 us (0.84)
  local copies, waits for them, and re-layouts: 12.1 us -> 0 us
  Pallas kernels: 52.9 us -> 55 us
    unnamed x28 -> x0, local copies, waits for them, and re-layouts: 12.1 us -> none
    pallas_call x1, Pallas kernels: 48.7 us -> 50.2 us  [run_step(): pl.pallas_call(functools.partial(step_kernel, owners, trainers, subs, cap...]
where the time goes in v4:
time: 55.9 us; the launch traced here: 55.6 us
  Pallas kernels  55 us (98%)
  between operations  0.65 us (1%)
    pallas_call x1, Pallas kernels, run_step(): pl.pallas_call(functools.partial(step_kernel, owners, trainers, subs, cap...  50.2 us
    pallas_call x1, Pallas kernels, finish(): pl.pallas_call(finish_kernel, out_shape=(jax.ShapeDtypeStruct((count, wid...  4.76 us

profile of v4, /device:TPU:0, one launch (start us, length us, event | category | flops | bytes accessed | tf_op | source)
XLA Modules:
  0.0 55.6 jit_solution(9504457013112650538)
XLA Ops:
  0.6 50.2 %step.1 = (s32[20,128]{1,0:T(8,128)}, bf16[4,1280,128]{2,1,0:T(8,128)(2,1)}, bf16[208,256]{1,0:T(8,128)(2,1)}) custom-call(s32[1,2560]{1,0:T(1,128)} %bitcast.18, s32[20,128]{1,0:T(8,128)} %bitcast.17, bf16[8192,128]{1,0:T(8,128)(2,1)} %table_h.1, bf16[2560,128]{1,0:T(8,128)(2,1)} %feats_h.1, s32[10,2048]{1,0:T(8,128)} %bitcast.13, s32[1,2048]{1,0:T(1,128)} %bitcast.19, ...), custom_call_target="tpu_custom_call" | custom-call | flops 4294967296 | bytes 62914560 | tf_op jit(solution)/shard_map/step/pallas_call | solution.py:353
  50.8 4.8 %finish.1 = (bf16[2560,128]{1,0:T(8,128)(2,1)}, bf16[32,256]{1,0:T(8,128)(2,1)}, bf16[32,256]{1,0:T(8,128)(2,1)}, bf16[1,64]{1,0:T(2,128)(2,1)}, bf16[64,172]{1,0:T(8,128)(2,1)}, /*index=5*/bf16[64,172]{1,0:T(8,128)(2,1)}) custom-call(s32[20,128]{1,0:T(8,128)} %get-tuple-element.15.slot_ref, bf16[5120,128]{1,0:T(8,128)(2,1)} %bitcast.12, ...), custom_call_target="tpu_custom_call" | custom-call | tf_op jit(solution)/shard_map/finish/pallas_call | solution.py:446
